TPU v7x, 512 devices: a whole 4x8x8 slice. The times are simulated.
512 devices in a mesh: expert: 128 (over y, z, core), dp: 4 (over x).
Axes of the slice: x: 4, y: 8, z: 8, core: 2. Of those that a mesh axis runs over, the one named last changes fastest.
Arguments:
- tokens: bfloat16 [32768, 2048], P(('expert', 'dp')), may hold values from -6 to 6
- grad_out: bfloat16 [32768, 2048], P(('expert', 'dp')), may hold values from -6 to 6
- route_expert: int32 [32768, 4], P(('expert', 'dp')), may hold values from 0 to 127, all different within a row; in each aligned block of 64 rows (0 to 63, 64 to 127, ...) at most 3 rows name the same one
- route_weight: bfloat16 [32768, 4], P(('expert', 'dp')), may hold values from 0.019897461 to 0.5
- gate_up_weight: bfloat16 [128, 2048, 768], P('expert', 'dp'), may hold values from -0.125 to 0.125
- down_weight: bfloat16 [128, 2048, 384], P('expert', 'dp'), may hold values from -0.3125 to 0.3125
Outputs:
- grad_tokens: bfloat16 [32768, 2048], P(('expert', 'dp'))
- grad_route: bfloat16 [32768, 4], P(('expert', 'dp'))
- grad_gate_up: float32 [128, 2048, 768], P('expert', 'dp')
- grad_down: float32 [128, 2048, 384], P('expert', 'dp')
Inputs may be any that keep to these rules, and one draw needn't show every extreme that they name: `route_expert`: each row names 4 different experts. In the 64 rows of one device (aligned blocks) no expert is named by more than 3 rows, a bound that some block reaches.
All inputs are finite; a program needn't handle non-finite values.
Results may differ from a plain program's by a relative error of at most 0.01.
Values may be sent and summed in bfloat16 or wider, within the bound.
A program may use at most 64 MiB of HBM per device.

v0:
```python
import jax
import jax.numpy as jnp
from jax import lax
from jax.sharding import PartitionSpec as P


def swish(value):
    return value * jax.nn.sigmoid(value)


def to_local(rows, group_count, local_count, capacity):
    tail = rows.shape[2:]
    shaped = rows.reshape((group_count, local_count, capacity) + tail)
    shaped = jnp.swapaxes(shaped, 0, 1)
    return shaped.reshape((local_count, group_count * capacity) + tail)


def to_groups(rows, group_count, local_count, capacity):
    tail = rows.shape[2:]
    shaped = rows.reshape((local_count, group_count, capacity) + tail)
    shaped = jnp.swapaxes(shaped, 0, 1)
    return shaped.reshape((group_count, local_count * capacity) + tail)


def on_device(tokens, grad_out, route_expert, route_weight, gate_up_weight, down_weight):
    token_count, model_width = tokens.shape
    route_count = route_expert.shape[1]
    group_count = lax.axis_size("expert")
    local_count = gate_up_weight.shape[0]
    hidden_width = down_weight.shape[2]
    expert_total = local_count * group_count
    capacity = min(token_count, (token_count * route_count + expert_total - 1) // expert_total + 1)
    slot_total = expert_total * capacity
    flat_expert = route_expert.reshape(-1)
    expert_ids = jnp.arange(expert_total, dtype=jnp.int32)
    onehot = (flat_expert[:, None] == expert_ids[None, :]).astype(jnp.int32)
    before = jnp.cumsum(onehot, axis=0) - onehot
    rank = jnp.sum(before * onehot, axis=1)
    slot_of = flat_expert * capacity + rank
    slot_ids = jnp.arange(slot_total, dtype=jnp.int32)
    placed = slot_ids[:, None] == slot_of[None, :]
    by_token = jnp.any(placed.reshape(slot_total, token_count, route_count), axis=2).astype(
        jnp.bfloat16
    )
    send_x = jnp.dot(by_token, tokens, preferred_element_type=jnp.float32).astype(jnp.bfloat16)
    send_dy = jnp.dot(by_token, grad_out, preferred_element_type=jnp.float32).astype(jnp.bfloat16)
    flat_weight = route_weight.reshape(-1).astype(jnp.float32)
    send_w = jnp.sum(jnp.where(placed, flat_weight[None, :], 0.0), axis=1).astype(jnp.bfloat16)
    recv_x, recv_dy, recv_w = (
        lax.all_to_all(
            send_x.reshape(group_count, local_count * capacity, model_width),
            "expert",
            split_axis=0,
            concat_axis=0,
            tiled=True,
        ),
        lax.all_to_all(
            send_dy.reshape(group_count, local_count * capacity, model_width),
            "expert",
            split_axis=0,
            concat_axis=0,
            tiled=True,
        ),
        lax.all_to_all(
            send_w.reshape(group_count, local_count * capacity),
            "expert",
            split_axis=0,
            concat_axis=0,
            tiled=True,
        ),
    )
    rows_x = to_local(recv_x, group_count, local_count, capacity)
    rows_dy = to_local(recv_dy, group_count, local_count, capacity)
    rows_w = to_local(recv_w, group_count, local_count, capacity)
    full_in, full_out = (
        lax.all_gather(gate_up_weight, "dp", axis=1, tiled=True),
        lax.all_gather(down_weight, "dp", axis=1, tiled=True),
    )
    pre = jnp.einsum("erd,edf->erf", rows_x, full_in, preferred_element_type=jnp.float32)
    gate_pre = pre[:, :, :hidden_width]
    up_pre = pre[:, :, hidden_width:]
    act = swish(gate_pre)
    hidden = (act * up_pre).astype(jnp.bfloat16)
    expert_out = jnp.einsum("erf,edf->erd", hidden, full_out, preferred_element_type=jnp.float32)
    route_grad = jnp.sum(rows_dy.astype(jnp.float32) * expert_out, axis=2).astype(jnp.bfloat16)
    scaled = (rows_w.astype(jnp.float32)[:, :, None] * rows_dy).astype(jnp.bfloat16)
    grad_hidden = jnp.einsum("erd,edf->erf", scaled, full_out, preferred_element_type=jnp.float32)
    sig = jax.nn.sigmoid(gate_pre)
    grad_gate = grad_hidden * up_pre * sig * (1.0 + gate_pre * (1.0 - sig))
    grad_up = grad_hidden * act
    grad_pre = jnp.concatenate([grad_gate, grad_up], axis=2).astype(jnp.bfloat16)
    rows_grad = jnp.einsum(
        "erf,edf->erd", grad_pre, full_in, preferred_element_type=jnp.float32
    ).astype(jnp.bfloat16)
    back_x, back_w = (
        lax.all_to_all(
            to_groups(rows_grad, group_count, local_count, capacity),
            "expert",
            split_axis=0,
            concat_axis=0,
            tiled=True,
        ),
        lax.all_to_all(
            to_groups(route_grad, group_count, local_count, capacity),
            "expert",
            split_axis=0,
            concat_axis=0,
            tiled=True,
        ),
    )
    back_x = back_x.reshape(slot_total, model_width)
    back_w = back_w.reshape(slot_total).astype(jnp.float32)
    grad_tokens = jnp.einsum(
        "st,sd->td", by_token, back_x, preferred_element_type=jnp.float32
    ).astype(jnp.bfloat16)
    grad_route = jnp.sum(jnp.where(placed, back_w[:, None], 0.0), axis=0)
    grad_route = grad_route.reshape(token_count, route_count).astype(jnp.bfloat16)
    all_x = lax.all_to_all(rows_x, "dp", split_axis=2, concat_axis=1, tiled=True)
    grad_gate_up = jnp.einsum(
        "erd,erf->edf",
        all_x,
        lax.all_gather(grad_pre, "dp", axis=1, tiled=True),
        preferred_element_type=jnp.float32,
    )
    summed = lax.psum_scatter(
        jnp.einsum("erd,erf->def", scaled, hidden, preferred_element_type=jnp.float32),
        "dp",
        scatter_dimension=0,
        tiled=True,
    )
    grad_down = jnp.swapaxes(summed, 0, 1)
    return (grad_tokens, grad_route, grad_gate_up, grad_down)


def solution(mesh):
    return jax.shard_map(
        on_device,
        mesh=mesh,
        in_specs=(
            P(("expert", "dp"), None),
            P(("expert", "dp"), None),
            P(("expert", "dp"), None),
            P(("expert", "dp"), None),
            P("expert", "dp", None),
            P("expert", "dp", None),
        ),
        out_specs=(
            P(("expert", "dp"), None),
            P(("expert", "dp"), None),
            P("expert", "dp", None),
            P("expert", "dp", None),
        ),
        check_vma=False,
    )
```

profile of v0, /device:TPU:1, one launch (start us, length us, event | category | flops | bytes accessed | tf_op | source)
XLA Modules:
  0.0 377.7 jit_solution(3388876717853676159)
XLA Ops:
  10.5 2.3 reshape.255
  12.8 18.6 %all-to-all-start.2 = ((bf16[128,3,2048]{2,1,0:T(4,128)(2,1)}), bf16[128,3,2048]{2,1,0:T(4,128)(2,1)S(1)}, u32[]{:S(2)}, u32[]{:S(2)}) async-start(bf16[128,3,2048]{2,1,0:T(4,128)(2,1)} %reshape.255), calls=%async_computation.2 | async-start | bytes 4194304 | tf_op jit(solution)/shard_map/all_to_all | solution.py:50
  31.4 1.8 convolution_convert_fusion.1
  33.2 5.1 %reshape.253 = bf16[128,3,2048]{2,1,0:T(4,128)(2,1)} reshape(bf16[384,2048]{1,0:T(8,128)(2,1)} %convolution_convert_fusion.1) | data formatting | bytes 3145728 | tf_op jit(solution)/shard_map/reshape | solution.py:58
  38.3 45.2 %all-to-all-done.2 = bf16[128,3,2048]{2,1,0:T(4,128)(2,1)S(1)} async-done(((bf16[128,3,2048]{2,1,0:T(4,128)(2,1)}), bf16[128,3,2048]{2,1,0:T(4,128)(2,1)S(1)}, u32[]{:S(2)}, u32[]{:S(2)}) %all-to-all-start.2) | async-done | bytes 1572896 | tf_op jit(solution)/shard_map/all_to_all | solution.py:50
  83.5 8.2 %all-to-all-start.1 = ((bf16[128,3,2048]{2,1,0:T(4,128)(2,1)}), bf16[128,3,2048]{2,1,0:T(4,128)(2,1)}, u32[]{:S(2)}, u32[]{:S(2)}) async-start(bf16[128,3,2048]{2,1,0:T(4,128)(2,1)} %reshape.253), calls=%async_computation.1 | async-start | bytes 4194304 | tf_op jit(solution)/shard_map/all_to_all | solution.py:57
  92.5 2.5 reshape.256
  95.1 48.5 %all-to-all-done.1 = bf16[128,3,2048]{2,1,0:T(4,128)(2,1)} async-done(((bf16[128,3,2048]{2,1,0:T(4,128)(2,1)}), bf16[128,3,2048]{2,1,0:T(4,128)(2,1)}, u32[]{:S(2)}, u32[]{:S(2)}) %all-to-all-start.1) | async-done | bytes 1572896 | tf_op jit(solution)/shard_map/all_to_all | solution.py:57
  143.6 5.2 %reshape.265 = f32[384,2048]{1,0:T(8,128)} reshape(bf16[128,3,2048]{2,1,0:T(4,128)(2,1)} %all-to-all-done.1) | data formatting | bytes 4718592 | tf_op jit(solution)/shard_map/convert_element_type | solution.py:86
  148.8 4.2 %fusion.16 = f32[1,384,768]{1,2,0:T(8,128)S(1)} fusion(bf16[384,2048]{1,0:T(8,128)(2,1)} %reshape.256, bf16[1,2048,768]{2,1,0:T(8,128)(2,1)} %all-gather.6.cloned.1.call-done), kind=kOutput, calls=%fused_computation.18 | convolution fusion | flops 1207959552 | bytes 5898240 | tf_op jit(solution)/shard_map/erd,edf->erf/dot_general | solution.py:79
  154.3 3.5 multiply_reduce_fusion
  158.6 7.8 %all-to-all-start.4 = ((bf16[128,1,3]{2,1,0:T(2,128)(2,1)}), bf16[128,1,3]{2,1,0:T(2,128)(2,1)S(1)}, u32[]{:S(2)}, u32[]{:S(2)}) async-start(bf16[128,1,3]{2,1,0:T(2,128)(2,1)} %convert_element_type.192), calls=%async_computation.4 | async-start | bytes 131072 | tf_op jit(solution)/shard_map/all_to_all | solution.py:103
  166.7 11.2 %all-to-all-done.4 = bf16[128,1,3]{2,1,0:T(2,128)(2,1)S(1)} async-done(((bf16[128,1,3]{2,1,0:T(2,128)(2,1)}), bf16[128,1,3]{2,1,0:T(2,128)(2,1)S(1)}, u32[]{:S(2)}, u32[]{:S(2)}) %all-to-all-start.4) | async-done | bytes 800 | tf_op jit(solution)/shard_map/all_to_all | solution.py:103
  179.4 5.7 %all-to-all-start = ((bf16[128,1,3]{2,1,0:T(2,128)(2,1)}), bf16[128,1,3]{2,1,0:T(2,128)(2,1)S(1)}, u32[]{:S(2)}, u32[]{:S(2)}) async-start(bf16[128,1,3]{2,1,0:T(2,128)(2,1)} %convert_element_type.191), calls=%async_computation | async-start | bytes 131072 | tf_op jit(solution)/shard_map/all_to_all | solution.py:64
  185.1 5.3 %reshape.264 = f32[1,384,1,1,1,1,2048]{6,1,5,4,3,2,0:T(8,128)} reshape(bf16[128,3,2048]{2,1,0:T(4,128)(2,1)} %all-to-all-done.1) | data formatting | bytes 4718592 | tf_op jit(solution)/shard_map/convert_element_type | solution.py:86
  190.4 6.3 %all-to-all-done = bf16[128,1,3]{2,1,0:T(2,128)(2,1)S(1)} async-done(((bf16[128,1,3]{2,1,0:T(2,128)(2,1)}), bf16[128,1,3]{2,1,0:T(2,128)(2,1)S(1)}, u32[]{:S(2)}, u32[]{:S(2)}) %all-to-all-start) | async-done | bytes 800 | tf_op jit(solution)/shard_map/all_to_all | solution.py:64
  197.1 3.9 %multiply_convert_fusion.3 = (bf16[1,384,384]{1,2,0:T(8,128)(2,1)S(1)}, bf16[1,384,384]{1,2,0:T(8,128)(2,1)S(1)}) fusion(f32[1,384,768]{1,2,0:T(8,128)} %copy-done.2, bf16[1,2048,384]{2,1,0:T(8,128)(2,1)} %all-gather.4.cloned.1.call-done, f32[1,384,1,1,1,1,2048]{6,1,5,4,3,2,0:T(8,128)} %reshape.264, f32[384]{0:T(512)S(1)} %reshape.263), kind=kOutput, calls=%fused_computation.26 | convolution fusion | flops 607469568 | bytes 6489600 | tf_op jit(solution)/shard_map/erd,edf->erf/dot_general | solution.py:87
  202.0 4.6 %convolution_bitcast_fusion = f32[2048,1,384]{0,2,1:T(8,128)} fusion(bf16[384,384]{0,1:T(8,128)(2,1)S(1)} %fusion.27, f32[1,384,1,1,1,1,2048]{6,1,5,4,3,2,0:T(8,128)} %reshape.264, f32[384]{0:T(512)S(1)} %reshape.263), kind=kOutput, calls=%fused_computation.6 | convolution fusion | flops 605552640 | bytes 6587904 | tf_op jit(solution)/shard_map/erd,erf->def/dot_general | solution.py:126
  206.7 2.5 reshape_transpose_reshape.10
  209.2 8.0 %copy.75 = bf16[1,384,2048]{1,0,2:T(2,128)(2,1)S(1)} copy(bf16[1,384,2048]{2,1,0:T(8,128)(2,1)} %reshape_transpose_reshape.10) | data formatting | bytes 3145728 | tf_op jit(solution)/shard_map/reshape;transpose;reshape | solution.py:15
  217.7 34.4 %reduce.10 = bf16[2048,384]{1,0:T(8,128)(2,1)} reduce(bf16[2048,1,384]{2,1,0:T(2,128)(2,1)S(1)} %bitcast.73, bf16[]{:T(256)} %broadcast.64), dimensions={1}, to_apply=%bitcast.54.reduce_sub_computation | reduce | bytes 3145730
  252.1 3.8 %reshape.279 = bf16[4,2,98304]{2,1,0:T(2,128)(2,1)} reshape(bf16[2048,384]{1,0:T(8,128)(2,1)} %reduce.10) | data formatting | bytes 3145728
  255.9 4.0 %all-to-all-start.5 = ((bf16[4,2,98304]{2,1,0:T(2,128)(2,1)}), bf16[4,2,98304]{2,1,0:T(2,128)(2,1)S(1)}, u32[]{:S(2)}, u32[]{:S(2)}) async-start(bf16[4,2,98304]{2,1,0:T(2,128)(2,1)} %reshape.279), calls=%async_computation.5 | async-start | bytes 3145728 | tf_op jit(solution)/shard_map/all_to_all | solution.py:118
  259.9 3.6 fusion.4
  263.5 2.3 reshape_transpose_reshape.4
  265.8 31.5 %all-to-all-done.5 = bf16[4,2,98304]{2,1,0:T(2,128)(2,1)S(1)} async-done(((bf16[4,2,98304]{2,1,0:T(2,128)(2,1)}), bf16[4,2,98304]{2,1,0:T(2,128)(2,1)S(1)}, u32[]{:S(2)}, u32[]{:S(2)}) %all-to-all-start.5) | async-done | bytes 1572896 | tf_op jit(solution)/shard_map/all_to_all | solution.py:118
  298.4 9.4 %all-to-all-start.3 = ((bf16[128,3,2048]{2,1,0:T(4,128)(2,1)}), bf16[128,3,2048]{2,1,0:T(4,128)(2,1)}, u32[]{:S(2)}, u32[]{:S(2)}) async-start(bf16[128,3,2048]{2,1,0:T(4,128)(2,1)} %reshape_transpose_reshape.4), calls=%async_computation.3 | async-start | bytes 4194304 | tf_op jit(solution)/shard_map/all_to_all | solution.py:96
  307.8 3.1 reshape.280
  314.8 44.8 %all-to-all-done.3 = bf16[128,3,2048]{2,1,0:T(4,128)(2,1)} async-done(((bf16[128,3,2048]{2,1,0:T(4,128)(2,1)}), bf16[128,3,2048]{2,1,0:T(4,128)(2,1)}, u32[]{:S(2)}, u32[]{:S(2)}) %all-to-all-start.3) | async-done | bytes 1572896 | tf_op jit(solution)/shard_map/all_to_all | solution.py:96
  359.6 3.9 %reshape.258 = bf16[384,2048]{1,0:T(8,128)(2,1)S(1)} reshape(bf16[128,3,2048]{2,1,0:T(4,128)(2,1)} %all-to-all-done.3) | data formatting | bytes 3145728 | tf_op jit(solution)/shard_map/reshape | solution.py:111
  364.6 4.2 %fusion.13 = f32[1,512,768]{2,1,0:T(8,128)} fusion(bf16[1536,512]{1,0:T(8,128)(2,1)S(1)} %bitcast.76, bf16[1,1536,768]{1,2,0:T(8,128)(2,1)} %all-gather.8.cloned.1.call-done), kind=kOutput, calls=%fused_computation.17 | convolution fusion | flops 1207959552 | bytes 5505024 | tf_op jit(solution)/shard_map/erd,erf->edf/dot_general | solution.py:119
  368.9 2.3 copy.78
  (63 shorter events, 15.9 us)
Async XLA Ops:
  7.2 2.7 copy-start
  7.2 2.5 copy-start.6
  7.2 141.6 %all-gather.6.cloned.1.call-start = ((), (), s32[]{:S(2)}) async-start(), calls=%async_computation.8 | async-start | bytes 3932160 | tf_op jit(solution)/shard_map/all_gather | solution.py:76
  12.8 18.6 %copy-start.5 = (bf16[64,2048]{1,0:T(8,128)(2,1)S(1)}, bf16[64,2048]{1,0:T(8,128)(2,1)}, u32[]{:S(2)}) copy-start(bf16[64,2048]{1,0:T(8,128)(2,1)} %param.7) | copy-start | bytes 786436
  12.8 70.7 %all-to-all-start.2 = ((bf16[128,3,2048]{2,1,0:T(4,128)(2,1)}), bf16[128,3,2048]{2,1,0:T(4,128)(2,1)S(1)}, u32[]{:S(2)}, u32[]{:S(2)}) async-start(bf16[128,3,2048]{2,1,0:T(4,128)(2,1)} %reshape.255), calls=%async_computation.2 | async-start | bytes 4194304 | tf_op jit(solution)/shard_map/all_to_all | solution.py:50
  83.5 60.0 %all-to-all-start.1 = ((bf16[128,3,2048]{2,1,0:T(4,128)(2,1)}), bf16[128,3,2048]{2,1,0:T(4,128)(2,1)}, u32[]{:S(2)}, u32[]{:S(2)}) async-start(bf16[128,3,2048]{2,1,0:T(4,128)(2,1)} %reshape.253), calls=%async_computation.1 | async-start | bytes 4194304 | tf_op jit(solution)/shard_map/all_to_all | solution.py:57
  91.8 62.5 %all-gather.4.cloned.1.call-start = ((), (), s32[]{:S(2)}) async-start(), calls=%async_computation.7 | async-start | bytes 1966080 | tf_op jit(solution)/shard_map/all_gather | solution.py:77
  153.0 1.0 copy-start.2
  154.2 12.2 %copy-start.7 = (bf16[64,4]{0,1:T(4,128)(2,1)S(1)}, bf16[64,4]{0,1:T(4,128)(2,1)}, u32[]{:S(2)}) copy-start(bf16[64,4]{0,1:T(4,128)(2,1)} %param.9) | copy-start | bytes 1540
  158.6 19.3 %all-to-all-start.4 = ((bf16[128,1,3]{2,1,0:T(2,128)(2,1)}), bf16[128,1,3]{2,1,0:T(2,128)(2,1)S(1)}, u32[]{:S(2)}, u32[]{:S(2)}) async-start(bf16[128,1,3]{2,1,0:T(2,128)(2,1)} %convert_element_type.192), calls=%async_computation.4 | async-start | bytes 131072 | tf_op jit(solution)/shard_map/all_to_all | solution.py:103
  179.4 17.3 %all-to-all-start = ((bf16[128,1,3]{2,1,0:T(2,128)(2,1)}), bf16[128,1,3]{2,1,0:T(2,128)(2,1)S(1)}, u32[]{:S(2)}, u32[]{:S(2)}) async-start(bf16[128,1,3]{2,1,0:T(2,128)(2,1)} %convert_element_type.191), calls=%async_computation | async-start | bytes 131072 | tf_op jit(solution)/shard_map/all_to_all | solution.py:64
  185.1 179.5 %all-gather.8.cloned.1.call-start = ((), (), s32[]{:S(2)}) async-start(), calls=%async_computation.9 | async-start | bytes 2949120 | tf_op jit(solution)/shard_map/all_gather | solution.py:122
  201.0 5.7 %copy-start.3 = (bf16[1,384,384]{1,2,0:T(8,128)(2,1)}, bf16[1,384,384]{1,2,0:T(8,128)(2,1)S(1)}, u32[]{:S(2)}) copy-start(bf16[1,384,384]{1,2,0:T(8,128)(2,1)S(1)} %get-tuple-element.30) | copy-start | bytes 884740
  201.0 5.7 %copy-start.4 = (bf16[1,384,384]{1,2,0:T(8,128)(2,1)}, bf16[1,384,384]{1,2,0:T(8,128)(2,1)S(1)}, u32[]{:S(2)}) copy-start(bf16[1,384,384]{1,2,0:T(8,128)(2,1)S(1)} %get-tuple-element.31) | copy-start | bytes 884740
  202.0 166.9 %reduce-scatter.2.cloned.1.call-start = ((), (), s32[]{:S(2)}) async-start(), calls=%async_computation.10 | async-start | bytes 3932160 | tf_op jit(solution)/shard_map/reduce_scatter | solution.py:125
  255.9 41.4 %all-to-all-start.5 = ((bf16[4,2,98304]{2,1,0:T(2,128)(2,1)}), bf16[4,2,98304]{2,1,0:T(2,128)(2,1)S(1)}, u32[]{:S(2)}, u32[]{:S(2)}) async-start(bf16[4,2,98304]{2,1,0:T(2,128)(2,1)} %reshape.279), calls=%async_computation.5 | async-start | bytes 3145728 | tf_op jit(solution)/shard_map/all_to_all | solution.py:118
  297.3 1.1 copy-start.1
  298.4 61.2 %all-to-all-start.3 = ((bf16[128,3,2048]{2,1,0:T(4,128)(2,1)}), bf16[128,3,2048]{2,1,0:T(4,128)(2,1)}, u32[]{:S(2)}, u32[]{:S(2)}) async-start(bf16[128,3,2048]{2,1,0:T(4,128)(2,1)} %reshape_transpose_reshape.4), calls=%async_computation.3 | async-start | bytes 4194304 | tf_op jit(solution)/shard_map/all_to_all | solution.py:96
Sparse Core Ops, SparseCore 0:
  10.1 50.3 all-gather.5
  94.7 32.6 all-gather.3
  202.1 32.9 all-gather.7
  237.8 59.1 reduce-scatter.1
where the time goes:
time: 379 us; the launch traced here: 378 us
  waiting for transfers between devices  189 us (50%)
  local copies, waits for them, and re-layouts  56.6 us (15%)
  starting transfers between devices  53.8 us (14%)
  other arithmetic  36.7 us (10%)
  matrix products  27.4 us (7%)
  between operations  14 us (4%)
    all_to_all x1, waiting for transfers between devices, on_device(): lax.all_to_all(send_dy.reshape(group_count, local_count * capacity, model...  48.5 us
    all_to_all x1, waiting for transfers between devices, on_device(): lax.all_to_all(send_x.reshape(group_count, local_count * capacity, model_...  45.2 us
    all_to_all x1, waiting for transfers between devices, on_device(): lax.all_to_all(to_groups(rows_grad, group_count, local_count, capacity),...  44.8 us
    unnamed x1, other arithmetic  34.4 us
    all_to_all x1, waiting for transfers between devices, on_device(): lax.all_to_all(rows_x, 'dp', split_axis=2, concat_axis=1, tiled=True)  31.5 us
    all_to_all x1, starting transfers between devices, on_device(): lax.all_to_all(send_x.reshape(group_count, local_count * capacity, model_...  18.6 us
    unnamed x24, local copies, waits for them, and re-layouts  14.7 us
    all_to_all x1, waiting for transfers between devices, on_device(): lax.all_to_all(to_groups(route_grad, group_count, local_count, capacity),...  11.2 us
  transfers between devices with their start and end apart: 10, of which 6 were waited for; matrix products, arithmetic and copies ran while one was open for 28% of the time, Pallas kernels for 0%

commit v1 on v0

v1 whole, which is shorter than its diff:
```python
import functools
import math

import jax
import jax.numpy as jnp
import numpy as np
from jax import lax
from jax.experimental import pallas as pl
from jax.experimental.pallas import tpu as pltpu
from jax.sharding import PartitionSpec as P

BF = jnp.bfloat16
F32 = jnp.float32
LANES = 128


def dot(a, b, dims=((1,), (0,))):
    return lax.dot_general(a, b, (dims, ((), ())), preferred_element_type=F32)


def kernel(n, cap, dpn, x_ref, dy_ref, info_ref, perm_ref, wgu_ref, wdn_ref,
           gt_ref, gr_ref, dgu_ref, ddn_ref,
           buf, infob, infor, sel, sb, xs, wgu, wdn, pre_s, gp_s, hid_s, ret, back,
           rs_out, rs_in, fin, finr, d0, d1, r0, r1,
           p0_s, p0_r, ag_s, ag_r, a2_s, a2_r, w_s, w_r, bk_s, bk_r, rs_s, rs_r, f_s, f_r,
           dp_s, dp_r):
    half_n = n // 2
    ch = 2 * n * cap
    tok, width = x_ref.shape
    wh = width // 2
    hid = wdn_ref.shape[1]
    blk = wgu_ref.shape[0]
    e = lax.axis_index("expert")
    d = lax.axis_index("dp")
    c = lax.rem(e, 2)
    z = lax.rem(e // 2, n)
    y = e // (2 * n)
    first = c == 0
    p = jnp.where(first, y, z)
    bm = jnp.where(first, z, y)

    def dev(yy, zz, cc):
        return {"expert": (yy * n + zz) * 2 + cc}

    def ring(k):
        at = lax.rem(p + k + n, n)
        return {"expert": jnp.where(first, (at * n + z) * 2, (y * n + at) * 2 + 1)}

    def other(b, cc):
        return {"expert": jnp.where(first, (y * n + b) * 2 + cc, (b * n + z) * 2 + cc)}

    sib = dev(y, z, 1 - c)
    right, left = lax.rem(d + 1, dpn), lax.rem(d + dpn - 1, dpn)

    def remote(src, dst, ss, rs, to):
        return pltpu.make_async_remote_copy(
            src_ref=src, dst_ref=dst, send_sem=ss, recv_sem=rs, device_id=to,
            device_id_type=pl.DeviceIdType.MESH)

    barrier = pltpu.get_barrier_semaphore()

    def greet(to):
        pl.semaphore_signal(barrier, inc=1, device_id=to, device_id_type=pl.DeviceIdType.MESH)

    @pl.loop(0, n)
    def _(b):
        for cc in range(2):
            @pl.when(jnp.logical_not(jnp.logical_and(b == z, c == cc)))
            def _():
                greet(dev(y, b, cc))

            @pl.when(b != y)
            def _():
                greet(dev(b, z, cc))

    if dpn > 1:
        greet({"dp": right})
        greet({"dp": left})
    pl.semaphore_wait(barrier, 4 * n - 3 + (2 if dpn > 1 else 0))

    pending = []

    def go(copy):
        copy.start()
        pending.append(copy)
        return copy

    psib = jnp.where(first, z, y)
    mine = pl.ds(pl.multiple_of(c * tok, tok), tok)
    mycol = pl.ds(pl.multiple_of(c * wh, wh), wh)
    hiscol = pl.ds(pl.multiple_of((1 - c) * wh, wh), wh)
    swap = [
        go(remote(info_ref.at[1 - c], infor, p0_s.at[2], p0_r.at[2], sib)),
        go(remote(x_ref.at[:, hiscol], buf.at[0, psib, mine], p0_s.at[0], p0_r.at[0], sib)),
        go(remote(dy_ref.at[:, hiscol], buf.at[1, psib, mine], p0_s.at[1], p0_r.at[1], sib)),
    ]

    if dpn > 1:
        wcopies = []
        for k, (src, dst) in enumerate(((wgu_ref, wgu), (wdn_ref, wdn))):
            wcopies.append(go(remote(src, dst.at[d], w_s.at[0, 0, k], w_r.at[0, 0, k], {"dp": right})))
            wcopies.append(go(remote(src, dst.at[d], w_s.at[0, 1, k], w_r.at[0, 1, k], {"dp": left})))

    buf[0, p, mine] = x_ref[:, mycol]
    buf[1, p, mine] = dy_ref[:, mycol]
    wgu[d] = wgu_ref[...]
    wdn[d] = wdn_ref[...]

    def ag(s, way, a):
        at = lax.rem(p - s + n, n) if way == 0 else lax.rem(p + s, n)
        if a == 2:
            ref = infob.at[at]
        elif s == half_n - 1:
            ref = buf.at[a, at, pl.ds(way * tok, tok)]
        else:
            ref = buf.at[a, at]
        return remote(ref, ref, ag_s.at[way, s, a], ag_r.at[way, s, a], ring(1 if way == 0 else -1))

    def ag_runs(s, way, a):
        return not (a == 2 and s == half_n - 1 and way == 1)

    swap[0].wait_recv()
    infob[p] = info_ref[c] + infor[...]
    copies = {}
    for a in (2, 0, 1):
        if a < 2:
            swap[a + 1].wait_recv()
        for way in range(2):
            if ag_runs(0, way, a):
                copies[0, way, a] = go(ag(0, way, a))
    for s in range(1, half_n):
        for a in (2, 0, 1):
            for way in range(2):
                copies[s - 1, way, a].wait_recv()
            for way in range(2):
                if ag_runs(s, way, a):
                    copies[s, way, a] = go(ag(s, way, a))
    copies[half_n - 1, 0, 2].wait_recv()

    base = (p * (n * 2 * ch) + 1).astype(F32)
    lanes = 2 * tok

    @pl.loop(0, n)
    def _(at):
        block = infob[at]
        rows = lax.broadcasted_iota(jnp.int32, (2 * n * ch, lanes), 0).astype(F32)
        picked = jnp.zeros((2 * n * ch, lanes), F32)
        scaled = jnp.zeros((2 * n * ch, lanes), F32)
        for k in range(4):
            hit = rows == (block[k:k + 1, :] - base)
            picked = jnp.where(hit, 1.0, picked)
            scaled = jnp.where(hit, block[4 + k:5 + k, :], scaled)
        cols = pl.ds(pl.multiple_of(at * lanes, lanes), lanes)
        sel[0, :, cols] = picked.astype(BF)
        sel[1, :, cols] = scaled.astype(BF)

    def dispatch(a):
        for way in range(2):
            copies[half_n - 1, way, a].wait_recv()

        @pl.loop(0, half_n)
        def _(g):
            places = (lax.rem(bm + g, n), lax.rem(bm + g + half_n, n))
            spans = [pl.ds(pl.multiple_of(b * (2 * ch), 2 * ch), 2 * ch) for b in places]
            lhs = jnp.concatenate([sel[a, span, :] for span in spans], axis=0)
            rows = dot(lhs, buf[a].reshape(n * lanes, wh)).astype(BF)
            for i, (b, span) in enumerate(zip(places, spans)):
                sb[a, span, :] = rows[i * 2 * ch:(i + 1) * 2 * ch]
                for cc in range(2):
                    src = sb.at[a, pl.ds(pl.multiple_of((b * 2 + cc) * ch, ch), ch)]
                    dst = xs.at[a, c, pl.ds(pl.multiple_of(bm * ch, ch), ch)]
                    own = jnp.logical_and(b == bm, c == cc)

                    @pl.when(own)
                    def _():
                        pltpu.make_async_copy(src, dst, a2_r.at[a, c, bm]).start()

                    @pl.when(jnp.logical_not(own))
                    def _():
                        remote(src, dst, a2_s.at[a, b * 2 + cc], a2_r.at[a, c, bm], other(b, cc)).start()

    def arrived(a):
        @pl.loop(0, n)
        def _(b):
            for h in range(2):
                ref = xs.at[a, h, pl.ds(pl.multiple_of(b * ch, ch), ch)]
                pltpu.make_async_copy(ref, ref, a2_r.at[a, h, b]).wait()

        xs[a, 1] = dot(perm_ref[...], xs[a, 1]).astype(BF)

    dispatch(0)
    dispatch(1)

    if dpn > 1:
        halfb = blk // 2
        for copy in wcopies:
            copy.wait_recv()
        wc2 = []
        for k, dst in enumerate((wgu, wdn)):
            top, low = dst.at[left, pl.ds(0, halfb)], dst.at[right, pl.ds(halfb, halfb)]
            wc2.append(go(remote(top, top, w_s.at[1, 0, k], w_r.at[1, 0, k], {"dp": right})))
            wc2.append(go(remote(low, low, w_s.at[1, 1, k], w_r.at[1, 1, k], {"dp": left})))

    def part(t):
        per = wh // blk
        return t // per, pl.ds(pl.multiple_of(lax.rem(t, per) * blk, blk), blk)

    arrived(0)
    if dpn > 1:
        for copy in wc2:
            copy.wait_recv()
    wgu_h = [wgu[h * dpn // 2:(h + 1) * dpn // 2].reshape(wh, 2 * hid) if dpn > 1
             else wgu[0, h * wh:(h + 1) * wh] for h in range(2)]
    wdn_h = [wdn[h * dpn // 2:(h + 1) * dpn // 2].reshape(wh, hid) if dpn > 1
             else wdn[0, h * wh:(h + 1) * wh] for h in range(2)]
    pre_s[...] = dot(xs[0, 0], wgu_h[0]) + dot(xs[0, 1], wgu_h[1])
    arrived(1)
    gh = dot(xs[1, 0], wdn_h[0]) + dot(xs[1, 1], wdn_h[1])
    gate, up = pre_s[:, :hid], pre_s[:, hid:]
    sig = jax.nn.sigmoid(gate)
    act = gate * sig
    hidden = (act * up).astype(BF)
    hid_s[...] = hidden
    gp_s[:, :hid] = (gh * up * sig * (1.0 + gate * (1.0 - sig))).astype(BF)
    gp_s[:, hid:] = (gh * act).astype(BF)
    weight_grad = jnp.sum(hidden.astype(F32) * gh, axis=1, keepdims=True)
    coarse = weight_grad.astype(BF).astype(F32)
    lane = lax.broadcasted_iota(jnp.int32, (n * ch, LANES), 1)
    spot = lane == lax.rem(e, LANES)
    ret[0, :, wh:] = jnp.where(spot, coarse, 0.0).astype(BF)
    fine = jnp.where(spot, weight_grad - coarse, 0.0).astype(BF)
    ret[1, :, wh:] = dot(perm_ref[...], fine).astype(BF)
    for h in range(2):
        rows = dot(gp_s[...], wgu_h[h], ((1,), (1,))).astype(BF)
        if h == 1:
            rows = dot(perm_ref[...], rows).astype(BF)
        ret[h, :, :wh] = rows

        @pl.loop(0, n)
        def _(i):
            b = lax.rem(bm + i, n)
            src = ret.at[h, pl.ds(pl.multiple_of(b * ch, ch), ch)]
            q = (z if h == 0 else y) * 2 + c
            dst = back.at[pl.ds(pl.multiple_of(q * ch, ch), ch)]
            own = jnp.logical_and(c == h, b == bm)

            @pl.when(own)
            def _():
                pltpu.make_async_copy(src, dst, bk_r.at[q]).start()

            @pl.when(jnp.logical_not(own))
            def _():
                to = dev(y, b, 0) if h == 0 else dev(b, z, 1)
                remote(src, dst, bk_s.at[h, b], bk_r.at[q], to).start()

    def weight_part(t):
        h, cols = part(t)
        return (dot(xs[0, h, :, cols], gp_s[...], ((0,), (0,))),
                dot(xs[1, h, :, cols], hid_s[...], ((0,), (0,))))

    if dpn > 1:
        both = ((0, {"dp": right}, 0), (1, {"dp": left}, halfb))
        far = weight_part(lax.rem(d + 2, dpn))
        d0[:, :2 * hid] = far[0].astype(BF)
        d0[:, 2 * hid:] = far[1].astype(BF)
        far_copies = [go(remote(d0.at[pl.ds(off, halfb)], r0.at[way], dp_s.at[0, way], dp_r.at[0, way], to))
                      for way, to, off in both]
    own_gu, own_dn = weight_part(d)
    dgu_ref[...] = own_gu
    ddn_ref[...] = own_dn

    @pl.loop(0, 2 * n)
    def _(q):
        ref = back.at[pl.ds(pl.multiple_of(q * ch, ch), ch)]
        pltpu.make_async_copy(ref, ref, bk_r.at[q]).wait()

    def share(t):
        cols = pl.ds(pl.multiple_of(t * lanes, lanes), lanes)
        return dot(sel[0, :, cols], back[...], ((0,), (0,)))

    def rs(s, way):
        rows = pl.ds(way * tok, tok) if s == 0 else pl.ds(0, lanes)
        return remote(rs_out.at[way, s, rows], rs_in.at[way, s, rows],
                      rs_s.at[way, s], rs_r.at[way, s], ring(1 if way == 0 else -1))

    whole = share(lax.rem(p + half_n, n)).astype(BF)
    rcopies = {}
    for way in range(2):
        rs_out[way, 0] = whole
        rcopies[0, way] = go(rs(0, way))

    def dp_second():
        out = []
        for way, to, off in both:
            gu, dn = weight_part(right if way == 0 else left)
            far_copies[way].wait_recv()
            d1[way, :, :2 * hid] = gu.astype(BF)
            d1[way, :, 2 * hid:] = dn.astype(BF)
            got = r0[way].astype(F32)
            here = slice(off, off + halfb)
            d1[way, here, :2 * hid] = (gu[here] + got[:, :2 * hid]).astype(BF)
            d1[way, here, 2 * hid:] = (dn[here] + got[:, 2 * hid:]).astype(BF)
            out.append(go(remote(d1.at[way], r1.at[way], dp_s.at[1, way], dp_r.at[1, way], to)))
        return out

    if dpn > 1:
        near = dp_second()
    for s in range(1, half_n):
        for way in range(2):
            mine_part = share(lax.rem(p + half_n - s if way == 0 else p + half_n + s, n))
            rcopies[s - 1, way].wait_recv()
            if s == 1:
                there = slice(way * tok, way * tok + tok)
                rs_out[way, s] = mine_part.astype(BF)
                rs_out[way, s, there] = (mine_part[there] + rs_in[way, 0, there].astype(F32)).astype(BF)
            else:
                rs_out[way, s] = (mine_part + rs_in[way, s - 1].astype(F32)).astype(BF)
            rcopies[s, way] = go(rs(s, way))
    total = share(p)
    last = half_n - 1
    for way in range(2):
        rcopies[last, way].wait_recv()
    if half_n == 1:
        for way in range(2):
            there = slice(way * tok, way * tok + tok)
            fin[there] = (total[there] + rs_in[way, 0, there].astype(F32)).astype(BF)
    else:
        fin[...] = (total + rs_in[0, last].astype(F32) + rs_in[1, last].astype(F32)).astype(BF)
    his = pl.ds(pl.multiple_of((1 - c) * tok, tok), tok)
    swapped = go(remote(fin.at[his], finr, f_s, f_r, sib))
    gt_ref[:, mycol] = fin[mine, :wh]
    swapped.wait_recv()
    gt_ref[:, hiscol] = finr[:, :wh]
    gr_ref[...] = fin[mine, wh:].astype(F32) + finr[:, wh:].astype(F32)

    if dpn > 1:
        for copy in near:
            copy.wait_recv()
        dgu_ref[...] += r1[0, :, :2 * hid].astype(F32) + r1[1, :, :2 * hid].astype(F32)
        ddn_ref[...] += r1[0, :, 2 * hid:].astype(F32) + r1[1, :, 2 * hid:].astype(F32)

    for copy in pending:
        copy.wait_send()

    @pl.loop(0, n)
    def _(b):
        for a in range(2):
            for cc in range(2):
                @pl.when(jnp.logical_not(jnp.logical_and(b == bm, c == cc)))
                def _():
                    ref = sb.at[a, pl.ds(pl.multiple_of((b * 2 + cc) * ch, ch), ch)]
                    pltpu.make_async_copy(ref, ref, a2_s.at[a, b * 2 + cc]).wait()
        for h in range(2):
            @pl.when(jnp.logical_not(jnp.logical_and(c == h, b == bm)))
            def _():
                ref = ret.at[h, pl.ds(pl.multiple_of(b * ch, ch), ch)]
                pltpu.make_async_copy(ref, ref, bk_s.at[h, b]).wait()


def on_device(n, dpn, tokens, grad_out, route_expert, route_weight, gate_up_weight, down_weight):
    tok, width = tokens.shape
    top = route_expert.shape[1]
    wh = width // 2
    blk, hid = down_weight.shape[1:]
    experts = 2 * n * n
    cap = min(tok, (tok * top + experts - 1) // experts + 1)
    ch = 2 * n * cap
    lanes = 2 * tok
    me = lax.axis_index("expert")
    c, z, y = me % 2, (me // 2) % n, me // (2 * n)

    chosen = route_expert.T
    flat = chosen.reshape(-1)
    owner = jnp.arange(top * tok, dtype=jnp.int32) % tok
    earlier = (flat[:, None] == flat[None, :]) & (owner[None, :] < owner[:, None])
    rank = jnp.sum(earlier.astype(jnp.int32), axis=1).reshape(top, tok)
    ec, ez, ey = chosen % 2, (chosen // 2) % n, chosen // (2 * n)
    by_y = ((ey * (2 * n) + ez * 2 + ec) * ch) + rank * (2 * n) + y * 2 + c + 1
    by_z = ((ez * (2 * n) + ey * 2 + ec) * ch) + rank * (2 * n) + z * 2 + c + 1
    weight = route_weight.T.astype(F32)
    info = jnp.stack([jnp.concatenate([code.astype(F32), weight], axis=0) for code in (by_y, by_z)])
    info = jnp.concatenate([jnp.where(c == 0, info, 0.0), jnp.where(c == 1, info, 0.0)], axis=2)

    at = np.arange(n * ch)
    hop = (at % (2 * n)) // 2 * ch + (at % ch) // (2 * n) * (2 * n) + at // ch * 2 + at % 2
    perm = np.zeros((n * ch, n * ch), np.float32)
    perm[at, hop] = 1.0
    perm = jnp.asarray(perm, BF)

    vm = pl.BlockSpec(memory_space=pltpu.VMEM)
    half_n = n // 2
    dma = pltpu.SemaphoreType.DMA
    all_rows = 2 * n * ch
    wx = wh + LANES
    cut = 3 * hid
    scratch = [
        pltpu.VMEM((2, n, lanes, wh), BF),
        pltpu.VMEM((n, 8, lanes), F32),
        pltpu.VMEM((8, lanes), F32),
        pltpu.VMEM((2, all_rows, n * lanes), BF),
        pltpu.VMEM((2, all_rows, wh), BF),
        pltpu.VMEM((2, 2, n * ch, wh), BF),
        pltpu.VMEM((dpn, blk, 2 * hid), BF),
        pltpu.VMEM((dpn, blk, hid), BF),
        pltpu.VMEM((n * ch, 2 * hid), F32),
        pltpu.VMEM((n * ch, 2 * hid), BF),
        pltpu.VMEM((n * ch, hid), BF),
        pltpu.VMEM((2, n * ch, wx), BF),
        pltpu.VMEM((all_rows, wx), BF),
        pltpu.VMEM((2, half_n, lanes, wx), BF),
        pltpu.VMEM((2, half_n, lanes, wx), BF),
        pltpu.VMEM((lanes, wx), BF),
        pltpu.VMEM((tok, wx), BF),
        pltpu.VMEM((blk, cut), BF),
        pltpu.VMEM((2, blk, cut), BF),
        pltpu.VMEM((2, blk // 2, cut), BF),
        pltpu.VMEM((2, blk, cut), BF),
        dma((3,)), dma((3,)),
        dma((2, half_n, 3)), dma((2, half_n, 3)),
        dma((2, 2 * n)), dma((2, 2, n)),
        dma((2, 2, 2)), dma((2, 2, 2)),
        dma((2, n)), dma((2 * n,)),
        dma((2, half_n)), dma((2, half_n)),
        dma, dma,
        dma((2, 2)), dma((2, 2)),
    ]
    grad_tokens, grad_w, grad_gu, grad_dn = pl.pallas_call(
        functools.partial(kernel, n, cap, dpn),
        out_shape=(
            jax.ShapeDtypeStruct((tok, width), BF),
            jax.ShapeDtypeStruct((tok, LANES), F32),
            jax.ShapeDtypeStruct((blk, 2 * hid), F32),
            jax.ShapeDtypeStruct((blk, hid), F32),
        ),
        in_specs=[vm] * 6,
        out_specs=(vm, vm, vm, vm),
        scratch_shapes=scratch,
        compiler_params=pltpu.CompilerParams(
            collective_id=0, has_side_effects=True, vmem_limit_bytes=60 * 1024 * 1024),
    )(tokens, grad_out, info, perm, gate_up_weight[0], down_weight[0])
    picked = route_expert[:, :, None] == jnp.arange(LANES, dtype=jnp.int32)[None, None, :]
    grad_route = jnp.sum(jnp.where(picked, grad_w[:, None, :], 0.0), axis=2)
    grad_route = (grad_route / route_weight.astype(F32)).astype(BF)
    return grad_tokens, grad_route, grad_gu[None], grad_dn[None]


def solution(mesh):
    n = math.isqrt(mesh.shape["expert"] // 2)
    return jax.shard_map(
        functools.partial(on_device, n, mesh.shape["dp"]),
        mesh=mesh,
        in_specs=(
            P(("expert", "dp"), None),
            P(("expert", "dp"), None),
            P(("expert", "dp"), None),
            P(("expert", "dp"), None),
            P("expert", "dp", None),
            P("expert", "dp", None),
        ),
        out_specs=(
            P(("expert", "dp"), None),
            P(("expert", "dp"), None),
            P("expert", "dp", None),
            P("expert", "dp", None),
        ),
        check_vma=False,
    )
```

time: 379 us -> 146 us (0.39)
  waiting for transfers between devices: 189 us -> 0 us
  Pallas kernels: 0 us -> 135 us
  starting transfers between devices: 53.8 us -> 0 us
  local copies, waits for them, and re-layouts: 56.6 us -> 6.14 us
  other arithmetic: 36.7 us -> 3.82 us
  matrix products: 27.4 us -> 0 us
  between operations: 14 us -> 0.73 us
    all_to_all x6 -> x0, waiting for transfers between devices: 188 us -> none  [the longest x1 48.5 us: on_device(): lax.all_to_all(send_dy.reshape(group_count, local_count * capacity, model...]
    pallas_call x0 -> x1, Pallas kernels: none -> 135 us  [on_device(): pl.pallas_call(functools.partial(kernel, n, cap, dpn), out_shape=(jax.Sha...]
    all_to_all x6 -> x0, starting transfers between devices: 53.7 us -> none  [the longest x1 18.6 us: on_device(): lax.all_to_all(send_x.reshape(group_count, local_count * capacity, model_...]
    unnamed x1 -> x0, other arithmetic: 34.4 us -> none
    dot_general x9 -> x0, matrix products: 27.4 us -> none  [the longest x1 4.62 us: on_device(): jnp.einsum('erd,erf->def', scaled, hidden, preferred_element_type=jnp.flo...]
    another operation x7 -> x0, local copies, waits for them, and re-layouts: 15.3 us -> none  [the longest x2 10.5 us: to_local(): return shaped.reshape((local_count, group_count * capacity) + tail)]
    convert_element_type x9 -> x0, local copies, waits for them, and re-layouts: 13 us -> none  [the longest x3 10.7 us: on_device(): rows_w.astype(jnp.float32)[:, :, None] * rows_dy]
    reshape x3 -> x0, local copies, waits for them, and re-layouts: 11.4 us -> none  [the longest x1 5.14 us: on_device(): send_dy.reshape(group_count, local_count * capacity, model_width)]
  transfers between devices with their start and end apart: 10 -> 0, of which waited for: 6 -> 0; matrix products, arithmetic and copies ran while one was open for 28% -> 0% of each run, Pallas kernels for 0% -> 0%
where the time goes in v1:
time: 146 us
  Pallas kernels  135 us (92%)
  local copies, waits for them, and re-layouts  6.14 us (4%)
  other arithmetic  3.82 us (3%)
    pallas_call x1, Pallas kernels, on_device(): pl.pallas_call(functools.partial(kernel, n, cap, dpn), out_shape=(jax.Sha...  135 us
    unnamed x9, local copies, waits for them, and re-layouts  5.29 us

profile of v1, /device:TPU:1, one launch (start us, length us, event | category | flops | bytes accessed | tf_op | source)
XLA Modules:
  0.0 146.1 jit_solution(13111179898513574382)
XLA Ops:
  0.6 0.0 copy-start.1
  0.6 0.0 copy-start.2
  0.7 0.8 eq.43
  1.5 0.2 convert_reduce_fusion
  1.7 0.1 mul.35
  1.8 0.7 add_convert_fusion.1
  2.5 0.7 convert_bitcast_fusion
  3.2 0.7 pad_maximum_fusion.1.info_ref
  3.9 135.4 %shard_map.102 = (bf16[64,2048]{1,0:T(8,128)(2,1)}, f32[64,128]{1,0:T(8,128)}, f32[512,768]{1,0:T(8,128)}, f32[512,384]{1,0:T(8,128)}) custom-call(bf16[64,2048]{1,0:T(8,128)(2,1)} %x_ref.1, bf16[64,2048]{1,0:T(8,128)(2,1)} %dy_ref.1, f32[2,8,128]{2,1,0:T(8,128)} %pad_maximum_fusion.1.info_ref, bf16[384,384]{1,0:T(8,128)(2,1)} %constant.110.clone.perm_ref, ...), custom_call_target="tpu_custom_call" | custom-call | tf_op jit(solution)/shard_map/pallas_call | solution.py:427
  139.3 0.0 copy-done.1
  139.3 0.9 select_reduce_fusion
  140.2 0.0 copy-done.2
  140.2 0.6 fusion.6
  140.8 1.7 %copy.15 = bf16[64,2048]{1,0:T(8,128)(2,1)} copy(bf16[64,2048]{1,0:T(8,128)(2,1)} %get-tuple-element.22) | data formatting | bytes 524288
  142.5 0.0 copy-start
  142.5 2.7 %copy.16 = f32[1,512,768]{2,1,0:T(8,128)} copy(f32[1,512,768]{2,1,0:T(8,128)} %bitcast.26) | data formatting | bytes 3145728
  145.2 0.0 copy-done
  145.2 0.9 copy.17
  (4 shorter events, 0.0 us)
Async XLA Ops:
  0.6 138.6 %copy-start.1 = (s32[64,4]{0,1:T(4,128)S(1)}, s32[64,4]{0,1:T(4,128)}, u32[]{:S(2)}) copy-start(s32[64,4]{0,1:T(4,128)} %param.9) | copy-start | bytes 3076
  0.6 139.6 %copy-start.2 = (bf16[64,4]{0,1:T(4,128)(2,1)S(1)}, bf16[64,4]{0,1:T(4,128)(2,1)}, u32[]{:S(2)}) copy-start(bf16[64,4]{0,1:T(4,128)(2,1)} %param.10) | copy-start | bytes 1540
  142.5 2.7 %copy-start = (f32[512,384]{1,0:T(8,128)S(1)}, f32[512,384]{1,0:T(8,128)}, u32[]{:S(2)}) copy-start(f32[512,384]{1,0:T(8,128)} %get-tuple-element.11) | copy-start | bytes 2359300

commit v2 on v1

v2 whole, which is shorter than its diff:
```python
import functools
import math

import jax
import jax.numpy as jnp
import numpy as np
from jax import lax
from jax.experimental import pallas as pl
from jax.experimental.pallas import tpu as pltpu
from jax.sharding import PartitionSpec as P

BF = jnp.bfloat16
F32 = jnp.float32
LANES = 128


def dot(a, b, dims=((1,), (0,))):
    return lax.dot_general(a, b, (dims, ((), ())), preferred_element_type=F32)


def kernel(n, cap, dpn, x_ref, dy_ref, route_ref, weight_ref, perm_ref, wgu_ref, wdn_ref,
           gt_ref, gr_ref, dgu_ref, ddn_ref,
           buf, info, infob, infor, sel, sb, xs, wgu, wdn, pre_s, gp_s, hid_s, ret, back,
           rs_out, rs_in, fin, finr, d0, d1, r0, r1, xa, gpa, g_out, g_in, g_col, g_part, g_all, g_fin,
           p0_s, p0_r, ag_s, ag_r, in_s, in_r, a2_s, a2_r, w_s, w_r, bk_s, bk_r, rs_s, rs_r,
           f_s, f_r, dp_s, dp_r, gb_s, gb_r, gs_s, gs_r, gf_s, gf_r, xb_s, xb_r, gp_sem_s, gp_sem_r):
    half_n = n // 2
    ch = 2 * n * cap
    tok, width = x_ref.shape
    wh = width // 2
    hid = wdn_ref.shape[1]
    blk = wgu_ref.shape[0]
    e = lax.axis_index("expert")
    d = lax.axis_index("dp")
    c = lax.rem(e, 2)
    z = lax.rem(e // 2, n)
    y = e // (2 * n)
    first = c == 0
    p = jnp.where(first, y, z)
    bm = jnp.where(first, z, y)

    def dev(yy, zz, cc):
        return {"expert": (yy * n + zz) * 2 + cc}

    def ring(k):
        at = lax.rem(p + k + n, n)
        return {"expert": jnp.where(first, (at * n + z) * 2, (y * n + at) * 2 + 1)}

    def other(b, cc):
        return {"expert": jnp.where(first, (y * n + b) * 2 + cc, (b * n + z) * 2 + cc)}

    sib = dev(y, z, 1 - c)
    right, left = lax.rem(d + 1, dpn), lax.rem(d + dpn - 1, dpn)

    def remote(src, dst, ss, rs, to):
        return pltpu.make_async_remote_copy(
            src_ref=src, dst_ref=dst, send_sem=ss, recv_sem=rs, device_id=to,
            device_id_type=pl.DeviceIdType.MESH)

    barrier = pltpu.get_barrier_semaphore()

    def greet(to):
        pl.semaphore_signal(barrier, inc=1, device_id=to, device_id_type=pl.DeviceIdType.MESH)

    @pl.loop(0, n)
    def _(b):
        for cc in range(2):
            @pl.when(jnp.logical_not(jnp.logical_and(b == z, c == cc)))
            def _():
                greet(dev(y, b, cc))

            @pl.when(b != y)
            def _():
                greet(dev(b, z, cc))

    greet({"dp": right})
    greet({"dp": left})

    experts = 2 * n * n
    lanes = 2 * tok
    base = (p * (n * 2 * ch) + 1).astype(F32)
    spot = lax.broadcasted_iota(jnp.int32, (tok, lanes), 1) - lax.broadcasted_iota(jnp.int32, (tok, lanes), 0)
    spread = jnp.where(spot == c * tok, 1.0, 0.0).astype(BF)
    lane = lax.broadcasted_iota(jnp.int32, (1, lanes), 1)
    held = jnp.logical_and(lane >= c * tok, lane < c * tok + tok)
    routes = dot(route_ref[...].astype(F32).astype(BF), spread)
    gates = dot(weight_ref[...], spread)
    routes = jnp.where(held, routes, -1.0)
    expert_row = lax.broadcasted_iota(jnp.int32, (experts, lanes), 0).astype(F32)
    hits = [routes[k:k + 1] == expert_row for k in range(4)]
    named = jnp.zeros((experts, lanes), F32)
    for hit in hits:
        named = jnp.where(hit, 1.0, named)
    earlier = (lax.broadcasted_iota(jnp.int32, (lanes, lanes), 0)
               < lax.broadcasted_iota(jnp.int32, (lanes, lanes), 1))
    before = dot(named.astype(BF), jnp.where(earlier, 1.0, 0.0).astype(BF))
    level = lax.broadcasted_iota(jnp.int32, (8, lanes), 0)
    picks = [jnp.zeros((8, lanes), F32), jnp.zeros((8, lanes), F32)]
    for k, hit in enumerate(hits):
        rank = jnp.sum(jnp.where(hit, before, 0.0), axis=0, keepdims=True)
        to = routes[k:k + 1].astype(jnp.int32)
        ec, ez, ey = lax.rem(to, 2), lax.rem(to // 2, n), to // (2 * n)
        by_y = (ey * (2 * n) + ez * 2 + ec) * ch + (y * 2 + c + 1)
        by_z = (ez * (2 * n) + ey * 2 + ec) * ch + (z * 2 + c + 1)
        for mode, place in enumerate((by_y, by_z)):
            code = jnp.where(held, place.astype(F32) + rank * (2.0 * n), 0.0)
            picks[mode] = jnp.where(level == k, code, picks[mode])
            picks[mode] = jnp.where(level == 4 + k, gates[k:k + 1], picks[mode])
    info[0] = picks[0]
    info[1] = picks[1]
    pl.semaphore_wait(barrier, 4 * n - 3 + 2)

    pending = []

    def go(copy):
        copy.start()
        pending.append(copy)
        return copy

    psib = jnp.where(first, z, y)
    mine = pl.ds(pl.multiple_of(c * tok, tok), tok)
    mycol = pl.ds(pl.multiple_of(c * wh, wh), wh)
    hiscol = pl.ds(pl.multiple_of((1 - c) * wh, wh), wh)
    swap = [
        go(remote(info.at[1 - c], infor, p0_s.at[2], p0_r.at[2], sib)),
        go(remote(x_ref.at[:, hiscol], buf.at[0, psib, mine], p0_s.at[0], p0_r.at[0], sib)),
        go(remote(dy_ref.at[:, hiscol], buf.at[1, psib, mine], p0_s.at[1], p0_r.at[1], sib)),
    ]

    wcopies = []
    for k, (src, dst) in enumerate(((wgu_ref, wgu), (wdn_ref, wdn))):
        wcopies.append(go(remote(src, dst.at[d], w_s.at[0, 0, k], w_r.at[0, 0, k], {"dp": right})))
        wcopies.append(go(remote(src, dst.at[d], w_s.at[0, 1, k], w_r.at[0, 1, k], {"dp": left})))
    buf[0, p, mine] = x_ref[:, mycol]
    buf[1, p, mine] = dy_ref[:, mycol]
    wgu[d] = wgu_ref[...]
    wdn[d] = wdn_ref[...]

    def ag(s, way, a):
        at = lax.rem(p - s + n, n) if way == 0 else lax.rem(p + s, n)
        ref = buf.at[a, at, pl.ds(way * tok, tok)] if s == half_n - 1 else buf.at[a, at]
        return remote(ref, ref, ag_s.at[way, s, a], ag_r.at[way, s, a], ring(1 if way == 0 else -1))

    copies = {}

    def gather(s):
        for a in range(2):
            if s == 0:
                swap[1 + a].wait_recv()
            for way in range(2):
                if s > 0:
                    copies[s - 1, way, a].wait_recv()
            for way in range(2):
                copies[s, way, a] = go(ag(s, way, a))

    swap[0].wait_recv()
    infob[p] = info[c] + infor[...]

    @pl.loop(1, n)
    def _(k):
        remote(infob.at[p], infob.at[p], in_s.at[k], in_r.at[p], ring(k)).start()

    gather(0)

    @pl.loop(1, n)
    def _(k):
        at = lax.rem(p + k, n)
        pltpu.make_async_copy(infob.at[at], infob.at[at], in_r.at[at]).wait()

    if half_n > 1:
        gather(1)

    @pl.loop(0, n)
    def _(at):
        block = infob[at]
        rows = lax.broadcasted_iota(jnp.int32, (2 * n * ch, lanes), 0).astype(F32)
        picked = jnp.zeros((2 * n * ch, lanes), F32)
        scaled = jnp.zeros((2 * n * ch, lanes), F32)
        for k in range(4):
            hit = rows == (block[k:k + 1, :] - base)
            picked = jnp.where(hit, 1.0, picked)
            scaled = jnp.where(hit, block[4 + k:5 + k, :], scaled)
        cols = pl.ds(pl.multiple_of(at * lanes, lanes), lanes)
        sel[0, :, cols] = picked.astype(BF)
        sel[1, :, cols] = scaled.astype(BF)

    for s in range(2, half_n):
        gather(s)

    def dispatch(a):
        for way in range(2):
            copies[half_n - 1, way, a].wait_recv()

        @pl.loop(0, half_n)
        def _(g):
            places = (lax.rem(bm + g, n), lax.rem(bm + g + half_n, n))
            spans = [pl.ds(pl.multiple_of(b * (2 * ch), 2 * ch), 2 * ch) for b in places]
            lhs = jnp.concatenate([sel[a, span, :] for span in spans], axis=0)
            rows = dot(lhs, buf[a].reshape(n * lanes, wh)).astype(BF)
            for i, (b, span) in enumerate(zip(places, spans)):
                sb[a, span, :] = rows[i * 2 * ch:(i + 1) * 2 * ch]
                for cc in range(2):
                    src = sb.at[a, pl.ds(pl.multiple_of((b * 2 + cc) * ch, ch), ch)]
                    dst = xs.at[a, c, pl.ds(pl.multiple_of(bm * ch, ch), ch)]
                    own = jnp.logical_and(b == bm, c == cc)

                    @pl.when(own)
                    def _():
                        pltpu.make_async_copy(src, dst, a2_r.at[a, c, bm]).start()

                    @pl.when(jnp.logical_not(own))
                    def _():
                        remote(src, dst, a2_s.at[a, b * 2 + cc], a2_r.at[a, c, bm], other(b, cc)).start()

    def arrived(a):
        @pl.loop(0, n)
        def _(b):
            for h in range(2):
                ref = xs.at[a, h, pl.ds(pl.multiple_of(b * ch, ch), ch)]
                pltpu.make_async_copy(ref, ref, a2_r.at[a, h, b]).wait()

        xs[a, 1] = dot(perm_ref[...], xs[a, 1]).astype(BF)

    dispatch(0)
    dispatch(1)
    halfb = blk // 2
    for copy in wcopies:
        copy.wait_recv()
    wc2 = []
    for k, dst in enumerate((wgu, wdn)):
        top, low = dst.at[left, pl.ds(0, halfb)], dst.at[right, pl.ds(halfb, halfb)]
        wc2.append(go(remote(top, top, w_s.at[1, 0, k], w_r.at[1, 0, k], {"dp": right})))
        wc2.append(go(remote(low, low, w_s.at[1, 1, k], w_r.at[1, 1, k], {"dp": left})))

    def part(t):
        per = wh // blk
        return t // per, pl.ds(pl.multiple_of(lax.rem(t, per) * blk, blk), blk)

    arrived(0)
    blocks = []
    for k in range(3):
        to = lax.rem(d + k + 1, dpn)
        h, cols = part(to)
        blocks.append(go(remote(xs.at[0, h, :, cols], xa.at[d], xb_s.at[k], xb_r.at[k], {"dp": to})))
    for copy in wc2:
        copy.wait_recv()
    wgu_h = [wgu[h * dpn // 2:(h + 1) * dpn // 2].reshape(wh, 2 * hid) for h in range(2)]
    wdn_h = [wdn[h * dpn // 2:(h + 1) * dpn // 2].reshape(wh, hid) for h in range(2)]
    pre_s[...] = dot(xs[0, 0], wgu_h[0]) + dot(xs[0, 1], wgu_h[1])
    arrived(1)
    gh = dot(xs[1, 0], wdn_h[0]) + dot(xs[1, 1], wdn_h[1])
    gate, up = pre_s[:, :hid], pre_s[:, hid:]
    sig = jax.nn.sigmoid(gate)
    act = gate * sig
    hidden = (act * up).astype(BF)
    hid_s[...] = hidden
    gp_s[:, :hid] = (gh * up * sig * (1.0 + gate * (1.0 - sig))).astype(BF)
    gp_s[:, hid:] = (gh * act).astype(BF)
    bulk = [go(remote(gp_s, gpa.at[d], gp_sem_s.at[0, way], gp_sem_r.at[0, way], {"dp": to}))
            for way, to in ((0, right), (1, left))]
    weight_grad = jnp.sum(hidden.astype(F32) * gh, axis=1, keepdims=True)
    ranks = weight_grad.reshape(n, cap, 2 * n, 1)
    lane = lax.broadcasted_iota(jnp.int32, (n, 2 * n, LANES), 2)
    packed = jnp.zeros((n, 2 * n, LANES), F32)
    for r in range(cap):
        packed = jnp.where(lane == r, ranks[:, r], packed)
    g_out[...] = packed.astype(BF)

    def down_part(t):
        h, cols = part(t)
        return dot(xs[1, h, :, cols], hid_s[...], ((0,), (0,)))

    both = ((0, {"dp": right}, 0), (1, {"dp": left}, halfb))
    d0[...] = down_part(lax.rem(d + 2, dpn)).astype(BF)
    far_copies = [go(remote(d0.at[pl.ds(off, halfb)], r0.at[way], dp_s.at[0, way], dp_r.at[0, way], to))
                  for way, to, off in both]

    for h in range(2):
        rows = dot(gp_s[...], wgu_h[h], ((1,), (1,))).astype(BF)
        if h == 1:
            rows = dot(perm_ref[...], rows).astype(BF)
        ret[h] = rows

        @pl.loop(0, n)
        def _(i):
            b = lax.rem(bm + i, n)
            src = ret.at[h, pl.ds(pl.multiple_of(b * ch, ch), ch)]
            q = (z if h == 0 else y) * 2 + c
            dst = back.at[pl.ds(pl.multiple_of(q * ch, ch), ch)]
            own = jnp.logical_and(c == h, b == bm)

            @pl.when(own)
            def _():
                pltpu.make_async_copy(src, dst, bk_r.at[q]).start()

            @pl.when(jnp.logical_not(own))
            def _():
                to = dev(y, b, 0) if h == 0 else dev(b, z, 1)
                remote(src, dst, bk_s.at[h, b], bk_r.at[q], to).start()

    @pl.loop(0, n)
    def _(b):
        own = jnp.logical_and(first, b == bm)

        @pl.when(own)
        def _():
            pltpu.make_async_copy(g_out.at[b], g_in.at[z * 2 + c], gb_r.at[z * 2 + c]).start()

        @pl.when(jnp.logical_not(own))
        def _():
            remote(g_out.at[b], g_in.at[z * 2 + c], gb_s.at[b], gb_r.at[z * 2 + c], dev(y, b, 0)).start()

    here_h, here_cols = part(d)
    ddn_ref[...] = down_part(d)
    dgu_ref[...] = dot(xs[0, here_h, :, here_cols], gp_s[...], ((0,), (0,)))
    near = []
    for way, to, off in both:
        dn = down_part(right if way == 0 else left)
        far_copies[way].wait_recv()
        d1[way] = dn.astype(BF)
        here = slice(off, off + halfb)
        d1[way, here] = (dn[here] + r0[way].astype(F32)).astype(BF)
        near.append(go(remote(d1.at[way], r1.at[way], dp_s.at[1, way], dp_r.at[1, way], to)))
    half_rows = n * ch // 2
    for copy in bulk:
        copy.wait_recv()
    top, low = gpa.at[left, pl.ds(0, half_rows)], gpa.at[right, pl.ds(half_rows, half_rows)]
    rest = [go(remote(top, top, gp_sem_s.at[1, 0], gp_sem_r.at[1, 0], {"dp": right})),
            go(remote(low, low, gp_sem_s.at[1, 1], gp_sem_r.at[1, 1], {"dp": left}))]

    def add_block(t):
        dgu_ref[...] += dot(xa[t], gpa[t], ((0,), (0,)))

    @pl.loop(0, 2 * n)
    def _(q):
        ref = back.at[pl.ds(pl.multiple_of(q * ch, ch), ch)]
        pltpu.make_async_copy(ref, ref, bk_r.at[q]).wait()

    def share(t):
        cols = pl.ds(pl.multiple_of(t * lanes, lanes), lanes)
        return dot(sel[0, :, cols], back[...], ((0,), (0,)))

    pieces = 4
    piece = lanes // pieces

    def rows_of(m):
        return slice(m * piece, (m + 1) * piece)

    def rs(s, way, m):
        rows = pl.ds(m * piece, piece)
        return remote(rs_out.at[way, s, rows], rs_in.at[way, s, rows],
                      rs_s.at[way, s, m], rs_r.at[way, s, m], ring(1 if way == 0 else -1))

    def rs_runs(s, way, m):
        return s > 0 or m // (pieces // 2) == way

    whole = share(lax.rem(p + half_n, n)).astype(BF)
    rcopies = {}
    for m in range(pieces):
        for way in range(2):
            if rs_runs(0, way, m):
                rs_out[way, 0, rows_of(m)] = whole[rows_of(m)]
                rcopies[0, way, m] = go(rs(0, way, m))

    @pl.when(first)
    def _():
        @pl.loop(0, 2 * n)
        def _(q):
            pltpu.make_async_copy(g_in.at[q], g_in.at[q], gb_r.at[q]).wait()

        lane3 = lax.broadcasted_iota(jnp.int32, (2 * n, 2 * n, LANES), 2)
        packed_in = g_in[...].astype(F32)
        for r in range(cap):
            value = jnp.sum(jnp.where(lane3 == r, packed_in, 0.0), axis=2, keepdims=True)
            g_col[:, r] = jnp.broadcast_to(value, (2 * n, 2 * n, lanes))

        @pl.loop(0, n)
        def _(i):
            at = lax.rem(p + i, n)
            block = infob[at]
            rows = lax.broadcasted_iota(jnp.int32, (2 * n * ch, lanes), 0).astype(F32)
            column = g_col[...].reshape(2 * n * ch, lanes)
            tile = jnp.zeros((8, lanes), F32)
            for k in range(4):
                hit = rows == (block[k:k + 1, :] - base)
                found = jnp.sum(jnp.where(hit, column, 0.0), axis=0, keepdims=True)
                tile = jnp.where(level == k, found, tile)
            g_part[at] = tile

            @pl.when(i == 0)
            def _():
                pltpu.make_async_copy(g_part.at[at], g_all.at[p], gs_r.at[p]).start()

            @pl.when(i != 0)
            def _():
                remote(g_part.at[at], g_all.at[p], gs_s.at[at], gs_r.at[p], dev(at, z, 0)).start()

    def taken(s, way, m, held_part):
        if not rs_runs(s, way, m):
            return held_part
        rcopies[s, way, m].wait_recv()
        return held_part + rs_in[way, s, rows_of(m)].astype(F32)

    for s in range(1, half_n):
        shares = [share(lax.rem(p + half_n - s if way == 0 else p + half_n + s, n)) for way in range(2)]
        for m in range(pieces):
            for way in range(2):
                rs_out[way, s, rows_of(m)] = taken(s - 1, way, m, shares[way][rows_of(m)]).astype(BF)
                rcopies[s, way, m] = go(rs(s, way, m))
        if s == 1:
            for copy in blocks:
                copy.wait_recv()
            add_block(left)
        if s == 2:
            add_block(right)
    total = share(p)
    for m in range(pieces):
        value = taken(half_n - 1, 0, m, total[rows_of(m)])
        fin[rows_of(m)] = taken(half_n - 1, 1, m, value).astype(BF)
    his = pl.ds(pl.multiple_of((1 - c) * tok, tok), tok)
    swapped = go(remote(fin.at[his], finr, f_s, f_r, sib))
    gt_ref[:, mycol] = fin[mine, :]

    @pl.when(first)
    def _():
        g_sum = jnp.zeros((8, lanes), F32)
        for src in range(n):
            pltpu.make_async_copy(g_all.at[src], g_all.at[src], gs_r.at[src]).wait()
            g_sum = g_sum + g_all[src]
        g_fin[...] = g_sum
        remote(g_fin, g_part.at[0], gf_s, gf_r, sib).start()

    swapped.wait_recv()
    gt_ref[:, hiscol] = finr[...]

    for copy in near:
        copy.wait_recv()
    ddn_ref[...] += r1[0].astype(F32) + r1[1].astype(F32)
    for copy in rest:
        copy.wait_recv()
    if half_n < 3:
        for copy in blocks[:3 if half_n < 2 else 0]:
            copy.wait_recv()
        for t in (left, right)[half_n - 1:]:
            add_block(t)
    add_block(lax.rem(d + 2, dpn))

    @pl.when(first)
    def _():
        pltpu.make_async_copy(g_fin, g_fin, gf_s).wait()

        @pl.loop(1, n)
        def _(i):
            at = lax.rem(p + i, n)
            pltpu.make_async_copy(g_part.at[at], g_part.at[at], gs_s.at[at]).wait()

    @pl.when(c == 1)
    def _():
        pltpu.make_async_copy(g_fin, g_fin, gf_r).wait()
        g_fin[...] = g_part[0]

    quotient = jnp.where(held, g_fin[0:4], 0.0) / jnp.where(held, info[0, 4:8], 1.0)
    gr_ref[...] = dot(quotient.astype(BF), spread, ((1,), (1,))).astype(BF)

    for copy in pending:
        copy.wait_send()

    @pl.loop(1, n)
    def _(k):
        pltpu.make_async_copy(infob.at[p], infob.at[p], in_s.at[k]).wait()

    @pl.loop(0, n)
    def _(b):
        for a in range(2):
            for cc in range(2):
                @pl.when(jnp.logical_not(jnp.logical_and(b == bm, c == cc)))
                def _():
                    ref = sb.at[a, pl.ds(pl.multiple_of((b * 2 + cc) * ch, ch), ch)]
                    pltpu.make_async_copy(ref, ref, a2_s.at[a, b * 2 + cc]).wait()
        for h in range(2):
            @pl.when(jnp.logical_not(jnp.logical_and(c == h, b == bm)))
            def _():
                ref = ret.at[h, pl.ds(pl.multiple_of(b * ch, ch), ch)]
                pltpu.make_async_copy(ref, ref, bk_s.at[h, b]).wait()
                if h == 0:
                    pltpu.make_async_copy(g_out.at[b], g_out.at[b], gb_s.at[b]).wait()


def on_device(n, dpn, tokens, grad_out, route_expert, route_weight, gate_up_weight, down_weight):
    tok, width = tokens.shape
    top = route_expert.shape[1]
    wh = width // 2
    blk, hid = down_weight.shape[1:]
    experts = 2 * n * n
    cap = min(tok, (tok * top + experts - 1) // experts + 1)
    ch = 2 * n * cap
    lanes = 2 * tok
    at = np.arange(n * ch)
    hop = (at % (2 * n)) // 2 * ch + (at % ch) // (2 * n) * (2 * n) + at // ch * 2 + at % 2
    perm = np.zeros((n * ch, n * ch), np.float32)
    perm[at, hop] = 1.0
    perm = jnp.asarray(perm, BF)

    vm = pl.BlockSpec(memory_space=pltpu.VMEM)
    half_n = n // 2
    dma = pltpu.SemaphoreType.DMA
    all_rows = 2 * n * ch
    wx = wh
    scratch = [
        pltpu.VMEM((2, n, lanes, wh), BF),
        pltpu.VMEM((2, 8, lanes), F32),
        pltpu.VMEM((n, 8, lanes), F32),
        pltpu.VMEM((8, lanes), F32),
        pltpu.VMEM((2, all_rows, n * lanes), BF),
        pltpu.VMEM((2, all_rows, wh), BF),
        pltpu.VMEM((2, 2, n * ch, wh), BF),
        pltpu.VMEM((dpn, blk, 2 * hid), BF),
        pltpu.VMEM((dpn, blk, hid), BF),
        pltpu.VMEM((n * ch, 2 * hid), F32),
        pltpu.VMEM((n * ch, 2 * hid), BF),
        pltpu.VMEM((n * ch, hid), BF),
        pltpu.VMEM((2, n * ch, wx), BF),
        pltpu.VMEM((all_rows, wx), BF),
        pltpu.VMEM((2, half_n, lanes, wx), BF),
        pltpu.VMEM((2, half_n, lanes, wx), BF),
        pltpu.VMEM((lanes, wx), BF),
        pltpu.VMEM((tok, wx), BF),
        pltpu.VMEM((blk, hid), BF),
        pltpu.VMEM((2, blk, hid), BF),
        pltpu.VMEM((2, blk // 2, hid), BF),
        pltpu.VMEM((2, blk, hid), BF),
        pltpu.VMEM((dpn, n * ch, blk), BF),
        pltpu.VMEM((dpn, n * ch, 2 * hid), BF),
        pltpu.VMEM((n, 2 * n, LANES), BF),
        pltpu.VMEM((2 * n, 2 * n, LANES), BF),
        pltpu.VMEM((2 * n, cap, 2 * n, lanes), F32),
        pltpu.VMEM((n, 8, lanes), F32),
        pltpu.VMEM((n, 8, lanes), F32),
        pltpu.VMEM((8, lanes), F32),
        dma((3,)), dma((3,)),
        dma((2, half_n, 2)), dma((2, half_n, 2)),
        dma((n,)), dma((n,)),
        dma((2, 2 * n)), dma((2, 2, n)),
        dma((2, 2, 2)), dma((2, 2, 2)),
        dma((2, n)), dma((2 * n,)),
        dma((2, half_n, 4)), dma((2, half_n, 4)),
        dma, dma,
        dma((2, 2)), dma((2, 2)),
        dma((n,)), dma((2 * n,)),
        dma((n,)), dma((n,)),
        dma, dma,
        dma((3,)), dma((3,)),
        dma((2, 2)), dma((2, 2)),
    ]
    grad_tokens, grad_w, grad_gu, grad_dn = pl.pallas_call(
        functools.partial(kernel, n, cap, dpn),
        out_shape=(
            jax.ShapeDtypeStruct((tok, width), BF),
            jax.ShapeDtypeStruct((top, tok), BF),
            jax.ShapeDtypeStruct((blk, 2 * hid), F32),
            jax.ShapeDtypeStruct((blk, hid), F32),
        ),
        in_specs=[vm] * 7,
        out_specs=(vm, vm, vm, vm),
        scratch_shapes=scratch,
        compiler_params=pltpu.CompilerParams(
            collective_id=0, has_side_effects=True, vmem_limit_bytes=60 * 1024 * 1024),
    )(tokens, grad_out, route_expert.T, route_weight.T, perm, gate_up_weight[0], down_weight[0])
    grad_route = grad_w.T
    return grad_tokens, grad_route, grad_gu[None], grad_dn[None]


def solution(mesh):
    n = math.isqrt(mesh.shape["expert"] // 2)
    return jax.shard_map(
        functools.partial(on_device, n, mesh.shape["dp"]),
        mesh=mesh,
        in_specs=(
            P(("expert", "dp"), None),
            P(("expert", "dp"), None),
            P(("expert", "dp"), None),
            P(("expert", "dp"), None),
            P("expert", "dp", None),
            P("expert", "dp", None),
        ),
        out_specs=(
            P(("expert", "dp"), None),
            P(("expert", "dp"), None),
            P("expert", "dp", None),
            P("expert", "dp", None),
        ),
        check_vma=False,
    )
```

time: 146 us -> 132 us (0.904)
  Pallas kernels: 135 us -> 124 us
  other arithmetic: 3.82 us -> 0 us
    pallas_call x1, Pallas kernels: 135 us -> 124 us  [on_device(): pl.pallas_call(functools.partial(kernel, n, cap, dpn), out_shape=(jax.Sha...]
    convert_element_type x3 -> x0, other arithmetic: 1.97 us -> none  [the longest x1 0.71 us: on_device(): code.astype(F32)]
    unnamed x9 -> x6, local copies, waits for them, and re-layouts: 5.29 us -> 6.52 us
where the time goes in v2:
time: 132 us
  Pallas kernels  124 us (94%)
  local copies, waits for them, and re-layouts  6.52 us (5%)
    pallas_call x1, Pallas kernels, on_device(): pl.pallas_call(functools.partial(kernel, n, cap, dpn), out_shape=(jax.Sha...  124 us
    unnamed x6, local copies, waits for them, and re-layouts  6.52 us

profile of v2, /device:TPU:1, one launch (start us, length us, event | category | flops | bytes accessed | tf_op | source)
XLA Modules:
  0.0 131.5 jit_solution(2471888283476394596)
XLA Ops:
  0.6 124.3 %shard_map.102 = (bf16[64,2048]{1,0:T(8,128)(2,1)}, bf16[4,64]{1,0:T(4,128)(2,1)}, f32[512,768]{1,0:T(8,128)}, f32[512,384]{1,0:T(8,128)}) custom-call(bf16[64,2048]{1,0:T(8,128)(2,1)} %x_ref.1, bf16[64,2048]{1,0:T(8,128)(2,1)} %dy_ref.1, s32[4,64]{1,0:T(4,128)} %bitcast.11, bf16[4,64]{1,0:T(4,128)(2,1)} %bitcast.12, ...), custom_call_target="tpu_custom_call" | custom-call | tf_op jit(solution)/shard_map/pallas_call | solution.py:555
  125.0 1.7 %copy.15 = bf16[64,2048]{1,0:T(8,128)(2,1)} copy(bf16[64,2048]{1,0:T(8,128)(2,1)} %get-tuple-element.16) | data formatting | bytes 524288
  126.7 1.2 copy.16
  127.9 0.0 copy-start
  127.9 2.7 %copy.17 = f32[1,512,768]{2,1,0:T(8,128)} copy(f32[1,512,768]{2,1,0:T(8,128)} %bitcast.7) | data formatting | bytes 3145728
  130.6 0.0 copy-done
  130.6 0.9 copy.18
Async XLA Ops:
  127.9 2.7 %copy-start = (f32[512,384]{1,0:T(8,128)S(1)}, f32[512,384]{1,0:T(8,128)}, u32[]{:S(2)}) copy-start(f32[512,384]{1,0:T(8,128)} %get-tuple-element.11) | copy-start | bytes 2359300

commit v3 on v2

--- a/solution.py
+++ b/solution.py
@@ -23,7 +23,7 @@
            buf, info, infob, infor, sel, sb, xs, wgu, wdn, pre_s, gp_s, hid_s, ret, back,
            rs_out, rs_in, fin, finr, d0, d1, r0, r1, xa, gpa, g_out, g_in, g_col, g_part, g_all, g_fin,
            p0_s, p0_r, ag_s, ag_r, in_s, in_r, a2_s, a2_r, w_s, w_r, bk_s, bk_r, rs_s, rs_r,
-           f_s, f_r, dp_s, dp_r, gb_s, gb_r, gs_s, gs_r, gf_s, gf_r, xb_s, xb_r, gp_sem_s, gp_sem_r):
+           f_s, f_r, dp_s, dp_r, gb_s, gb_r, gs_s, gs_r, gf_s, gf_r, xb_s, xb_r, gp_sem_s, gp_sem_r, perm, ld, last_in, last_r, dgu_v, out_s, fs_s, fs_r):
     half_n = n // 2
     ch = 2 * n * cap
     tok, width = x_ref.shape
@@ -57,6 +57,8 @@
             src_ref=src, dst_ref=dst, send_sem=ss, recv_sem=rs, device_id=to,
             device_id_type=pl.DeviceIdType.MESH)
 
+    fetch = [pltpu.make_async_copy(src, dst, at_sem) for src, dst, at_sem in (
+        (wgu_ref, wgu.at[d], ld.at[0]), (wdn_ref, wdn.at[d], ld.at[1]), (perm_ref, perm, ld.at[2]))]
     barrier = pltpu.get_barrier_semaphore()
 
     def greet(to):
@@ -75,6 +77,8 @@
 
     greet({"dp": right})
     greet({"dp": left})
+    for copy in fetch:
+        copy.start()
 
     experts = 2 * n * n
     lanes = 2 * tok
@@ -121,20 +125,37 @@
     mine = pl.ds(pl.multiple_of(c * tok, tok), tok)
     mycol = pl.ds(pl.multiple_of(c * wh, wh), wh)
     hiscol = pl.ds(pl.multiple_of((1 - c) * wh, wh), wh)
+    def first_step(a, way, h):
+        k = 1 if way == 0 else -1
+        if h == 0:
+            to, at, cols = ring(k), p, mycol
+        else:
+            zz, yy = lax.rem(z + k + n, n), lax.rem(y + k + n, n)
+            to = {"expert": jnp.where(first, (y * n + zz) * 2 + 1, (yy * n + z) * 2)}
+            at, cols = psib, hiscol
+        src = (x_ref, dy_ref)[a].at[:, cols]
+        return remote(src, buf.at[a, at, mine], fs_s.at[way, a, h], fs_r.at[way, a, c], to)
+
+    slots = go(remote(info.at[1 - c], infor, p0_s.at[2], p0_r.at[2], sib))
+    for a in range(2):
+        for way in range(2):
+            for h in range(2):
+                go(first_step(a, way, h))
     swap = [
-        go(remote(info.at[1 - c], infor, p0_s.at[2], p0_r.at[2], sib)),
+        slots,
         go(remote(x_ref.at[:, hiscol], buf.at[0, psib, mine], p0_s.at[0], p0_r.at[0], sib)),
         go(remote(dy_ref.at[:, hiscol], buf.at[1, psib, mine], p0_s.at[1], p0_r.at[1], sib)),
     ]
 
     wcopies = []
-    for k, (src, dst) in enumerate(((wgu_ref, wgu), (wdn_ref, wdn))):
+    for k, dst in enumerate((wgu, wdn)):
+        fetch[k].wait()
+        src = dst.at[d]
         wcopies.append(go(remote(src, dst.at[d], w_s.at[0, 0, k], w_r.at[0, 0, k], {"dp": right})))
         wcopies.append(go(remote(src, dst.at[d], w_s.at[0, 1, k], w_r.at[0, 1, k], {"dp": left})))
     buf[0, p, mine] = x_ref[:, mycol]
     buf[1, p, mine] = dy_ref[:, mycol]
-    wgu[d] = wgu_ref[...]
-    wdn[d] = wdn_ref[...]
+    fetch[2].wait()
 
     def ag(s, way, a):
         at = lax.rem(p - s + n, n) if way == 0 else lax.rem(p + s, n)
@@ -145,10 +166,13 @@
 
     def gather(s):
         for a in range(2):
-            if s == 0:
-                swap[1 + a].wait_recv()
             for way in range(2):
-                if s > 0:
+                if s == 1:
+                    at = lax.rem(p + n - 1 if way == 0 else p + 1, n)
+                    for m in range(2):
+                        ref = buf.at[a, at, pl.ds(m * tok, tok)]
+                        pltpu.make_async_copy(ref, ref, fs_r.at[way, a, m]).wait()
+                else:
                     copies[s - 1, way, a].wait_recv()
             for way in range(2):
                 copies[s, way, a] = go(ag(s, way, a))
@@ -160,15 +184,12 @@
     def _(k):
         remote(infob.at[p], infob.at[p], in_s.at[k], in_r.at[p], ring(k)).start()
 
-    gather(0)
+    gather(1)
 
     @pl.loop(1, n)
     def _(k):
         at = lax.rem(p + k, n)
         pltpu.make_async_copy(infob.at[at], infob.at[at], in_r.at[at]).wait()
-
-    if half_n > 1:
-        gather(1)
 
     @pl.loop(0, n)
     def _(at):
@@ -188,6 +209,7 @@
         gather(s)
 
     def dispatch(a):
+        swap[1 + a].wait_recv()
         for way in range(2):
             copies[half_n - 1, way, a].wait_recv()
 
@@ -219,7 +241,7 @@
                 ref = xs.at[a, h, pl.ds(pl.multiple_of(b * ch, ch), ch)]
                 pltpu.make_async_copy(ref, ref, a2_r.at[a, h, b]).wait()
 
-        xs[a, 1] = dot(perm_ref[...], xs[a, 1]).astype(BF)
+        xs[a, 1] = dot(perm[...], xs[a, 1]).astype(BF)
 
     dispatch(0)
     dispatch(1)
@@ -278,7 +300,7 @@
     for h in range(2):
         rows = dot(gp_s[...], wgu_h[h], ((1,), (1,))).astype(BF)
         if h == 1:
-            rows = dot(perm_ref[...], rows).astype(BF)
+            rows = dot(perm[...], rows).astype(BF)
         ret[h] = rows
 
         @pl.loop(0, n)
@@ -312,7 +334,14 @@
 
     here_h, here_cols = part(d)
     ddn_ref[...] = down_part(d)
-    dgu_ref[...] = dot(xs[0, here_h, :, here_cols], gp_s[...], ((0,), (0,)))
+    dgu_v[...] = dot(xs[0, here_h, :, here_cols], gp_s[...], ((0,), (0,)))
+    half_rows = n * ch // 2
+    for copy in bulk:
+        copy.wait_recv()
+    top, low = gpa.at[left, pl.ds(0, half_rows)], gpa.at[right, pl.ds(half_rows, half_rows)]
+    rest = [go(remote(top, top, gp_sem_s.at[1, 0], gp_sem_r.at[1, 0], {"dp": right})),
+            go(remote(low, low, gp_sem_s.at[1, 1], gp_sem_r.at[1, 1], {"dp": left}))]
+
     near = []
     for way, to, off in both:
         dn = down_part(right if way == 0 else left)
@@ -321,15 +350,8 @@
         here = slice(off, off + halfb)
         d1[way, here] = (dn[here] + r0[way].astype(F32)).astype(BF)
         near.append(go(remote(d1.at[way], r1.at[way], dp_s.at[1, way], dp_r.at[1, way], to)))
-    half_rows = n * ch // 2
-    for copy in bulk:
-        copy.wait_recv()
-    top, low = gpa.at[left, pl.ds(0, half_rows)], gpa.at[right, pl.ds(half_rows, half_rows)]
-    rest = [go(remote(top, top, gp_sem_s.at[1, 0], gp_sem_r.at[1, 0], {"dp": right})),
-            go(remote(low, low, gp_sem_s.at[1, 1], gp_sem_r.at[1, 1], {"dp": left}))]
-
     def add_block(t):
-        dgu_ref[...] += dot(xa[t], gpa[t], ((0,), (0,)))
+        dgu_v[...] += dot(xa[t], gpa[t], ((0,), (0,)))
 
     @pl.loop(0, 2 * n)
     def _(q):
@@ -348,8 +370,16 @@
 
     def rs(s, way, m):
         rows = pl.ds(m * piece, piece)
-        return remote(rs_out.at[way, s, rows], rs_in.at[way, s, rows],
-                      rs_s.at[way, s, m], rs_r.at[way, s, m], ring(1 if way == 0 else -1))
+        k = 1 if way == 0 else -1
+        if s < half_n - 1:
+            return remote(rs_out.at[way, s, rows], rs_in.at[way, s, rows],
+                          rs_s.at[way, s, m], rs_r.at[way, s, m], ring(k))
+        at = lax.rem(p + k + n, n)
+        owner = m * 2 // pieces
+        to = {"expert": jnp.where(first, (at * n + z) * 2, (y * n + at) * 2) + owner}
+        i = m % (pieces // 2)
+        return remote(rs_out.at[way, s, rows], last_in.at[c, way, pl.ds(i * piece, piece)],
+                      rs_s.at[way, s, m], last_r.at[c, way, i], to)
 
     def rs_runs(s, way, m):
         return s > 0 or m // (pieces // 2) == way
@@ -413,13 +443,24 @@
             add_block(left)
         if s == 2:
             add_block(right)
-    total = share(p)
-    for m in range(pieces):
-        value = taken(half_n - 1, 0, m, total[rows_of(m)])
-        fin[rows_of(m)] = taken(half_n - 1, 1, m, value).astype(BF)
+    fin[...] = share(p).astype(BF)
     his = pl.ds(pl.multiple_of((1 - c) * tok, tok), tok)
     swapped = go(remote(fin.at[his], finr, f_s, f_r, sib))
-    gt_ref[:, mycol] = fin[mine, :]
+    swapped.wait_recv()
+
+    def finish(h, way, i):
+        there = last_in.at[h, way, pl.ds(i * piece, piece)]
+        pltpu.make_async_copy(there, there, last_r.at[h, way, i]).wait()
+        return last_in[h, way, i * piece:(i + 1) * piece].astype(F32)
+
+    for i in range(pieces // 2):
+        span = slice(i * piece, (i + 1) * piece)
+        for h, cols, begun in ((c, mycol, fin[pl.ds(pl.multiple_of(c * tok + i * piece, piece), piece), :]),
+                               (1 - c, hiscol, finr[span])):
+            value = begun.astype(F32)
+            for way in range(2):
+                value = value + finish(h, way, i)
+            gt_ref[span, cols] = value.astype(BF)
 
     @pl.when(first)
     def _():
@@ -430,20 +471,16 @@
         g_fin[...] = g_sum
         remote(g_fin, g_part.at[0], gf_s, gf_r, sib).start()
 
-    swapped.wait_recv()
-    gt_ref[:, hiscol] = finr[...]
-
+    for copy in rest:
+        copy.wait_recv()
+    if half_n < 3:
+        add_block(right)
+    add_block(lax.rem(d + 2, dpn))
+    leaving = pltpu.make_async_copy(dgu_v, dgu_ref, out_s)
+    leaving.start()
     for copy in near:
         copy.wait_recv()
     ddn_ref[...] += r1[0].astype(F32) + r1[1].astype(F32)
-    for copy in rest:
-        copy.wait_recv()
-    if half_n < 3:
-        for copy in blocks[:3 if half_n < 2 else 0]:
-            copy.wait_recv()
-        for t in (left, right)[half_n - 1:]:
-            add_block(t)
-    add_block(lax.rem(d + 2, dpn))
 
     @pl.when(first)
     def _():
@@ -462,6 +499,7 @@
     quotient = jnp.where(held, g_fin[0:4], 0.0) / jnp.where(held, info[0, 4:8], 1.0)
     gr_ref[...] = dot(quotient.astype(BF), spread, ((1,), (1,))).astype(BF)
 
+    leaving.wait()
     for copy in pending:
         copy.wait_send()
 
@@ -484,6 +522,27 @@
                 pltpu.make_async_copy(ref, ref, bk_s.at[h, b]).wait()
                 if h == 0:
                     pltpu.make_async_copy(g_out.at[b], g_out.at[b], gb_s.at[b]).wait()
+
+
+def hand_over(*refs):
+    count = len(refs) // 4
+    ins, outs, rooms = refs[:count], refs[count:2 * count], refs[2 * count:3 * count]
+    sems = refs[3 * count:]
+    moves = []
+    for src, dst, room, (come, leave) in zip(ins, outs, rooms, [(s.at[0], s.at[1]) for s in sems]):
+        rows = src.shape[0]
+        step = rows // 4 if rows >= 64 else rows
+        for i in range(0, rows, step):
+            part = pl.ds(i, step)
+            moves.append((pltpu.make_async_copy(src.at[part], room.at[part], come.at[i // step]),
+                          pltpu.make_async_copy(room.at[part], dst.at[part], leave.at[i // step])))
+    for come, _ in moves:
+        come.start()
+    for come, leave in moves:
+        come.wait()
+        leave.start()
+    for _, leave in moves:
+        leave.wait()
 
 
 def on_device(n, dpn, tokens, grad_out, route_expert, route_weight, gate_up_weight, down_weight):
@@ -551,6 +610,13 @@
         dma, dma,
         dma((3,)), dma((3,)),
         dma((2, 2)), dma((2, 2)),
+        pltpu.VMEM((n * ch, n * ch), BF),
+        dma((3,)),
+        pltpu.VMEM((2, 2, tok, wx), BF),
+        dma((2, 2, 2)),
+        pltpu.VMEM((blk, 2 * hid), F32),
+        dma,
+        dma((2, 2, 2)), dma((2, 2, 2)),
     ]
     grad_tokens, grad_w, grad_gu, grad_dn = pl.pallas_call(
         functools.partial(kernel, n, cap, dpn),
@@ -560,13 +626,23 @@
             jax.ShapeDtypeStruct((blk, 2 * hid), F32),
             jax.ShapeDtypeStruct((blk, hid), F32),
         ),
-        in_specs=[vm] * 7,
-        out_specs=(vm, vm, vm, vm),
+        in_specs=[vm] * 4 + [pl.BlockSpec(memory_space=pl.ANY)] * 3,
+        out_specs=(vm, vm, pl.BlockSpec(memory_space=pl.ANY), vm),
         scratch_shapes=scratch,
         compiler_params=pltpu.CompilerParams(
             collective_id=0, has_side_effects=True, vmem_limit_bytes=60 * 1024 * 1024),
     )(tokens, grad_out, route_expert.T, route_weight.T, perm, gate_up_weight[0], down_weight[0])
     grad_route = grad_w.T
+    results = (grad_tokens, grad_gu, grad_dn)
+    hbm = pl.BlockSpec(memory_space=pl.ANY)
+    grad_tokens, grad_gu, grad_dn = pl.pallas_call(
+        hand_over,
+        out_shape=tuple(jax.ShapeDtypeStruct(r.shape, r.dtype) for r in results),
+        in_specs=[hbm] * 3,
+        out_specs=(hbm,) * 3,
+        scratch_shapes=[pltpu.VMEM(r.shape, r.dtype) for r in results] + [dma((2, 4))] * 3,
+        compiler_params=pltpu.CompilerParams(vmem_limit_bytes=60 * 1024 * 1024),
+    )(*results)
     return grad_tokens, grad_route, grad_gu[None], grad_dn[None]
 
 

time: 132 us -> 127 us (0.962)
  local copies, waits for them, and re-layouts: 6.52 us -> 0.57 us
    unnamed x6 -> x3, local copies, waits for them, and re-layouts: 6.52 us -> 0.57 us
    pallas_call x0 -> x1, Pallas kernels: none -> 3.1 us  [on_device(): pl.pallas_call(hand_over, out_shape=tuple((jax.ShapeDtypeStruct(r.shape,...]
    pallas_call x1, Pallas kernels: 124 us -> 122 us  [on_device(): pl.pallas_call(functools.partial(kernel, n, cap, dpn), out_shape=(jax.Sha...]
where the time goes in v3:
time: 127 us; the launch traced here: 126 us
  Pallas kernels  125 us (98%)
    pallas_call x1, Pallas kernels, on_device(): pl.pallas_call(functools.partial(kernel, n, cap, dpn), out_shape=(jax.Sha...  122 us
    pallas_call x1, Pallas kernels, on_device(): pl.pallas_call(hand_over, out_shape=tuple((jax.ShapeDtypeStruct(r.shape,...  3.1 us

profile of v3, /device:TPU:1, one launch (start us, length us, event | category | flops | bytes accessed | tf_op | source)
XLA Modules:
  0.0 126.4 jit_solution(7210329277273833047)
XLA Ops:
  0.6 122.1 %shard_map.102 = (bf16[64,2048]{1,0:T(8,128)(2,1)}, bf16[4,64]{1,0:T(4,128)(2,1)}, f32[512,768]{1,0:T(8,128)}, f32[512,384]{1,0:T(8,128)}) custom-call(bf16[64,2048]{1,0:T(8,128)(2,1)} %x_ref.1, bf16[64,2048]{1,0:T(8,128)(2,1)} %dy_ref.1, s32[4,64]{1,0:T(4,128)} %bitcast.9, bf16[4,64]{1,0:T(4,128)(2,1)} %bitcast.10, ...), custom_call_target="tpu_custom_call" | custom-call | tf_op jit(solution)/shard_map/pallas_call | solution.py:621
  122.7 0.0 copy-start
  122.8 3.1 %shard_map.103 = (bf16[64,2048]{1,0:T(8,128)(2,1)}, f32[512,768]{1,0:T(8,128)}, f32[512,384]{1,0:T(8,128)}) custom-call(bf16[64,2048]{1,0:T(8,128)(2,1)} %get-tuple-element.11.refs_0_, f32[512,768]{1,0:T(8,128)} %get-tuple-element.12.refs_1_, f32[512,384]{1,0:T(8,128)} %get-tuple-element.13.refs_2_), custom_call_target="tpu_custom_call" | custom-call | tf_op jit(solution)/shard_map/pallas_call | solution.py:638
  125.9 0.0 copy-done
  125.9 0.6 copy.12
Async XLA Ops:
  122.7 3.1 %copy-start = (bf16[4,64]{1,0:T(4,128)(2,1)S(1)}, bf16[4,64]{1,0:T(4,128)(2,1)}, u32[]{:S(2)}) copy-start(bf16[4,64]{1,0:T(4,128)(2,1)} %get-tuple-element.15) | copy-start | bytes 1540

commit v4 on v3

--- a/solution.py
+++ b/solution.py
@@ -280,6 +280,38 @@
     gp_s[:, hid:] = (gh * act).astype(BF)
     bulk = [go(remote(gp_s, gpa.at[d], gp_sem_s.at[0, way], gp_sem_r.at[0, way], {"dp": to}))
             for way, to in ((0, right), (1, left))]
+    for h in range(2):
+        rows = dot(gp_s[...], wgu_h[h], ((1,), (1,))).astype(BF)
+        if h == 1:
+            rows = dot(perm[...], rows).astype(BF)
+        ret[h] = rows
+
+        @pl.loop(0, n)
+        def _(i):
+            b = lax.rem(bm + i, n)
+            src = ret.at[h, pl.ds(pl.multiple_of(b * ch, ch), ch)]
+            q = (z if h == 0 else y) * 2 + c
+            dst = back.at[pl.ds(pl.multiple_of(q * ch, ch), ch)]
+            own = jnp.logical_and(c == h, b == bm)
+
+            @pl.when(own)
+            def _():
+                pltpu.make_async_copy(src, dst, bk_r.at[q]).start()
+
+            @pl.when(jnp.logical_not(own))
+            def _():
+                to = dev(y, b, 0) if h == 0 else dev(b, z, 1)
+                remote(src, dst, bk_s.at[h, b], bk_r.at[q], to).start()
+
+    def down_part(t):
+        h, cols = part(t)
+        return dot(xs[1, h, :, cols], hid_s[...], ((0,), (0,)))
+
+    both = ((0, {"dp": right}, 0), (1, {"dp": left}, halfb))
+    d0[...] = down_part(lax.rem(d + 2, dpn)).astype(BF)
+    far_copies = [go(remote(d0.at[pl.ds(off, halfb)], r0.at[way], dp_s.at[0, way], dp_r.at[0, way], to))
+                  for way, to, off in both]
+
     weight_grad = jnp.sum(hidden.astype(F32) * gh, axis=1, keepdims=True)
     ranks = weight_grad.reshape(n, cap, 2 * n, 1)
     lane = lax.broadcasted_iota(jnp.int32, (n, 2 * n, LANES), 2)
@@ -287,38 +319,6 @@
     for r in range(cap):
         packed = jnp.where(lane == r, ranks[:, r], packed)
     g_out[...] = packed.astype(BF)
-
-    def down_part(t):
-        h, cols = part(t)
-        return dot(xs[1, h, :, cols], hid_s[...], ((0,), (0,)))
-
-    both = ((0, {"dp": right}, 0), (1, {"dp": left}, halfb))
-    d0[...] = down_part(lax.rem(d + 2, dpn)).astype(BF)
-    far_copies = [go(remote(d0.at[pl.ds(off, halfb)], r0.at[way], dp_s.at[0, way], dp_r.at[0, way], to))
-                  for way, to, off in both]
-
-    for h in range(2):
-        rows = dot(gp_s[...], wgu_h[h], ((1,), (1,))).astype(BF)
-        if h == 1:
-            rows = dot(perm[...], rows).astype(BF)
-        ret[h] = rows
-
-        @pl.loop(0, n)
-        def _(i):
-            b = lax.rem(bm + i, n)
-            src = ret.at[h, pl.ds(pl.multiple_of(b * ch, ch), ch)]
-            q = (z if h == 0 else y) * 2 + c
-            dst = back.at[pl.ds(pl.multiple_of(q * ch, ch), ch)]
-            own = jnp.logical_and(c == h, b == bm)
-
-            @pl.when(own)
-            def _():
-                pltpu.make_async_copy(src, dst, bk_r.at[q]).start()
-
-            @pl.when(jnp.logical_not(own))
-            def _():
-                to = dev(y, b, 0) if h == 0 else dev(b, z, 1)
-                remote(src, dst, bk_s.at[h, b], bk_r.at[q], to).start()
 
     @pl.loop(0, n)
     def _(b):

time: 127 us -> 127 us (level)
  no operation moved by 1% of the time
where the time goes in v4:
time: 127 us; the launch traced here: 126 us
  Pallas kernels  125 us (98%)
    pallas_call x1, Pallas kernels, on_device(): pl.pallas_call(functools.partial(kernel, n, cap, dpn), out_shape=(jax.Sha...  122 us
    pallas_call x1, Pallas kernels, on_device(): pl.pallas_call(hand_over, out_shape=tuple((jax.ShapeDtypeStruct(r.shape,...  3.1 us

profile of v4, /device:TPU:1, one launch (start us, length us, event | category | flops | bytes accessed | tf_op | source)
XLA Modules:
  0.0 126.5 jit_solution(6017394183968891499)
XLA Ops:
  0.6 122.1 %shard_map.102 = (bf16[64,2048]{1,0:T(8,128)(2,1)}, bf16[4,64]{1,0:T(4,128)(2,1)}, f32[512,768]{1,0:T(8,128)}, f32[512,384]{1,0:T(8,128)}) custom-call(bf16[64,2048]{1,0:T(8,128)(2,1)} %x_ref.1, bf16[64,2048]{1,0:T(8,128)(2,1)} %dy_ref.1, s32[4,64]{1,0:T(4,128)} %bitcast.9, bf16[4,64]{1,0:T(4,128)(2,1)} %bitcast.10, ...), custom_call_target="tpu_custom_call" | custom-call | tf_op jit(solution)/shard_map/pallas_call | solution.py:621
  122.8 0.0 copy-start
  122.8 3.1 %shard_map.103 = (bf16[64,2048]{1,0:T(8,128)(2,1)}, f32[512,768]{1,0:T(8,128)}, f32[512,384]{1,0:T(8,128)}) custom-call(bf16[64,2048]{1,0:T(8,128)(2,1)} %get-tuple-element.11.refs_0_, f32[512,768]{1,0:T(8,128)} %get-tuple-element.12.refs_1_, f32[512,384]{1,0:T(8,128)} %get-tuple-element.13.refs_2_), custom_call_target="tpu_custom_call" | custom-call | tf_op jit(solution)/shard_map/pallas_call | solution.py:638
  125.9 0.0 copy-done
  125.9 0.6 copy.12
Async XLA Ops:
  122.8 3.1 %copy-start = (bf16[4,64]{1,0:T(4,128)(2,1)S(1)}, bf16[4,64]{1,0:T(4,128)(2,1)}, u32[]{:S(2)}) copy-start(bf16[4,64]{1,0:T(4,128)(2,1)} %get-tuple-element.15) | copy-start | bytes 1540
